TPU v7x, 32 devices: a whole 2x2x4 slice. The times are simulated.
32 devices in a mesh: seq: 16 (over z, y, x), eig: 2 (over core).
Axes of the slice: x: 2, y: 2, z: 4, core: 2. Of those that a mesh axis runs over, the one named last changes fastest.
Arguments:
- train_in: bfloat16 [2048, 5120], P('seq'), may hold values from -6 to 6
- train_out: bfloat16 [2048, 13824], P('seq'), may hold values from -6 to 6
- query_in: bfloat16 [16, 5120], P('seq'), may hold values from -6 to 6
- query_out: bfloat16 [16, 13824], P('seq'), may hold values from -6 to 6
- input_basis: bfloat16 [5120, 5120], P('seq', 'eig'), may hold values from -0.078125 to 0.078125
- output_basis: bfloat16 [13824, 6912], P('seq', 'eig'), may hold values from -0.0546875 to 0.0546875
- corrected: bfloat16 [5120, 6912], P('seq', 'eig'), may hold values from 0.0099487305 to 10
- train_seq: int32 [2048], P('seq'), may hold values from 0 to 1
- query_order: int32 [16], P('seq'), may hold values from 0 to 15, each once
Outputs:
- scores: float32 [32, 16], P('seq')
Inputs may be any that keep to these rules, and one draw needn't show every extreme that they name: query_order holds every number of 0 to 15 once, so each query has 1 token.
All inputs are finite; a program needn't handle non-finite values.
Results may differ from a plain program's by a relative error of at most 0.025.
Values may be sent and summed in bfloat16 or wider, within the bound.
No kernel may reach another device: no remote copies, remote signals or barrier semaphores. Data moves between devices by JAX's collectives and lax.ppermute only.
A program may use at most 192 MiB of HBM per device.

v0:
```python
import math

import jax
import jax.numpy as jnp
from jax import lax
from jax.sharding import PartitionSpec as P

DIN = 5120
EIGOUT = 6912
TOK_DEV = 128
SEQ_DEV = 2
QUERIES = 16


DAMPING = 0.1


def body(
    train_in,
    train_out,
    query_in,
    query_out,
    input_basis,
    output_basis,
    corrected,
    train_seq,
    query_order,
):
    query_rows = query_in.shape[0]
    groups = lax.axis_size("seq")
    block_in, block_qin, block_out, block_qout = (
        lax.all_to_all(train_in, "seq", split_axis=1, concat_axis=0, tiled=True),
        lax.all_to_all(query_in, "seq", split_axis=1, concat_axis=0, tiled=True),
        lax.all_to_all(train_out, "seq", split_axis=1, concat_axis=0, tiled=True),
        lax.all_to_all(query_out, "seq", split_axis=1, concat_axis=0, tiled=True),
    )
    labels = (
        (query_order % QUERIES)[:, None] == jnp.arange(QUERIES, dtype=jnp.int32)[None, :]
    ).astype(jnp.float32)
    rotated_in = lax.psum_scatter(
        jnp.dot(block_in, input_basis, preferred_element_type=jnp.float32).astype(jnp.bfloat16),
        "seq",
        scatter_dimension=0,
        tiled=True,
    ).astype(jnp.float32)
    rotated_out = lax.psum_scatter(
        jnp.dot(block_out, output_basis, preferred_element_type=jnp.float32).astype(jnp.bfloat16),
        "seq",
        scatter_dimension=0,
        tiled=True,
    ).astype(jnp.float32)
    rotated_in = rotated_in.astype(jnp.bfloat16)
    rotated_out = rotated_out.astype(jnp.bfloat16)
    placed = jnp.zeros((groups * query_rows, QUERIES), jnp.float32)
    placed = lax.dynamic_update_slice_in_dim(placed, labels, lax.axis_index("seq") * query_rows, 0)
    summed = (
        lax.psum(
            jnp.dot(block_qin, input_basis, preferred_element_type=jnp.float32).astype(
                jnp.bfloat16
            ),
            "seq",
        ).astype(jnp.float32),
        lax.psum(
            jnp.dot(block_qout, output_basis, preferred_element_type=jnp.float32).astype(
                jnp.bfloat16
            ),
            "seq",
        ).astype(jnp.float32),
        lax.psum(placed.astype(jnp.bfloat16), "seq").astype(jnp.float32),
    )
    query_a = summed[0].astype(jnp.bfloat16)
    query_b = summed[1].astype(jnp.bfloat16)
    query_hot = summed[2]
    full_a, full_qa = (
        lax.all_gather(rotated_in, "eig", axis=1, tiled=True),
        lax.all_gather(query_a, "eig", axis=1, tiled=True),
    )
    query_float = query_b.astype(jnp.float32)
    width_out = rotated_out.shape[1]
    masks = [
        jnp.where((train_seq == member)[:, None], rotated_out, jnp.zeros_like(rotated_out))
        for member in range(SEQ_DEV)
    ]
    initial = jnp.zeros((SEQ_DEV, full_qa.shape[0], width_out), jnp.float32)
    piece = lax.all_gather(corrected, "seq", axis=0, tiled=True)
    row_count = piece.shape[0]
    block_rows = row_count
    while block_rows > 1280 and block_rows % 2 == 0:
        block_rows = block_rows // 2
    totals = [initial[member] for member in range(SEQ_DEV)]
    for offset in range(0, row_count, block_rows):
        a_cols = lax.dynamic_slice_in_dim(full_a, offset, block_rows, 1)
        q_cols = lax.dynamic_slice_in_dim(full_qa, offset, block_rows, 1)
        damped = piece[offset : offset + block_rows].astype(jnp.float32) + DAMPING
        for member in range(SEQ_DEV):
            raw_grad = lax.dot_general(
                a_cols, masks[member], (((0,), (0,)), ((), ())), preferred_element_type=jnp.float32
            )
            scaled = (raw_grad / damped).astype(jnp.bfloat16)
            totals[member] = totals[member] + jnp.dot(
                q_cols, scaled, preferred_element_type=jnp.float32
            )
    running = jnp.stack(totals)
    per_token = jnp.sum(running * query_float[None, :, :], axis=2)
    partial_value = jnp.sum(per_token[:, :, None] * query_hot[None, :, :], axis=1)
    summed_scores = lax.psum(partial_value, "eig")
    factor = 1.0 / math.sqrt(DIN * EIGOUT * (TOK_DEV / SEQ_DEV) * (full_qa.shape[0] / QUERIES))
    return summed_scores * factor


def solution(mesh):
    placed = (
        P("seq", None),
        P("seq", None),
        P("seq", None),
        P("seq", None),
        P("seq", "eig"),
        P("seq", "eig"),
        P("seq", "eig"),
        P("seq"),
        P("seq"),
    )
    return jax.shard_map(
        body, mesh=mesh, in_specs=placed, out_specs=P("seq", None), check_vma=False
    )
```

profile of v0, /device:TPU:0, one launch (start us, length us, event | category | flops | bytes accessed | tf_op | source)
XLA Modules:
  0.0 1118.3 jit_solution(5207300112391916118)
XLA Ops:
  6.5 1.9 copy.25
  8.4 40.6 %all_to_all.72 = bf16[128,16,320]{0,2,1:T(8,128)(2,1)S(1)} all-to-all(bf16[128,16,320]{0,2,1:T(8,128)(2,1)S(1)} %bitcast.38), channel_id=1, replica_groups=mesh['seq'=16,'eig'=2] {'seq'}, dimensions={1} | all-to-all | bytes 2621440 | tf_op jit(solution)/shard_map/all_to_all | solution.py:32
  49.1 8.2 convolution_convert_fusion.1
  57.3 0.7 copy-done.5
  58.0 0.1 reduce
  58.1 0.1 all_to_all.66
  58.2 0.5 broadcast.68
  58.7 0.7 reduce.2
  59.4 0.7 reshape.42
  60.1 3.5 all-to-all-start
  63.6 0.2 reduce.1
  63.7 0.1 all_to_all.67
  63.8 0.8 reduce.3
  64.7 0.7 reshape.44
  65.4 14.3 %all-to-all-done = bf16[16,2,160]{2,1,0:T(2,128)(2,1)S(1)} async-done(((bf16[16,2,160]{2,1,0:T(2,128)(2,1)}), bf16[16,2,160]{2,1,0:T(2,128)(2,1)S(1)}, u32[]{:S(2)}, u32[]{:S(2)}) %all-to-all-start) | async-done | bytes 10272 | tf_op jit(solution)/shard_map/all_to_all | solution.py:33
  79.7 3.4 all-to-all-start.3
  83.1 6.0 copy.27
  89.1 2.0 all-to-all-done.3
  91.1 4.9 all-to-all-start.2
  96.0 0.0 all-reduce.3.cloned.1.call-start
  96.1 0.1 reshape.43
  96.2 1.0 convolution_convert_fusion.3
  97.2 0.1 reshape.45
  97.3 4.2 convolution_convert_fusion.2
  101.6 215.7 %reduce-scatter.3.cloned.1.call-done = bf16[128,2560]{1,0:T(8,128)(2,1)} async-done(((bf16[2048,2560]{1,0:T(8,128)(2,1)}), bf16[128,2560]{1,0:T(8,128)(2,1)}) %reduce-scatter.3.cloned.1.call-update) | async-done | bytes 655376 | tf_op jit(solution)/shard_map/reduce_scatter | solution.py:40
  317.4 0.5 reduce-scatter.5.cloned.1.call-start
  317.9 21.7 %convolution_convert_fusion = bf16[2048,3456]{1,0:T(8,128)(2,1)} fusion(bf16[864,3456]{1,0:T(8,128)(2,1)} %param.14, bf16[128,16,864]{0,2,1:T(8,128)(2,1)} %all-to-all-done.2), kind=kOutput, calls=%fused_computation.12 | convolution fusion | flops 12237668352 | bytes 23666688 | tf_op jit(solution)/shard_map/dot_general | solution.py:47
  339.7 0.5 all-gather.5.cloned.1.call-update
  340.9 44.2 %psum.30 = bf16[16,16]{1,0:T(8,128)(2,1)S(1)} all-reduce(bf16[16,16]{1,0:T(8,128)(2,1)S(1)} %dynamic_update_slice.3), channel_id=1, replica_groups=mesh['seq'=16,'eig'=2] {'seq'}, use_global_device_ids=true, to_apply=%region_5.6 | all-reduce | flops 256 | bytes 1024 | tf_op jit(solution)/shard_map/psum | solution.py:69
  385.1 0.6 convert_element_type.95
  385.7 48.3 %all-reduce.3.cloned.1.call-done = (bf16[16,2560]{1,0:T(8,128)(2,1)}, bf16[16,3456]{1,0:T(8,128)(2,1)}) async-done(((bf16[16,2560]{1,0:T(8,128)(2,1)}, bf16[16,3456]{1,0:T(8,128)(2,1)}), (bf16[16,2560]{1,0:T(8,128)(2,1)}, bf16[16,3456]{1,0:T(8,128)(2,1)})) %all-reduce.3.cloned.1.call-update) | async-done | bytes 192528 | tf_op jit(solution)/shard_map/psum | solution.py:57
  434.1 1.6 convert_element_type.92
  435.7 2.4 all_gather.9
  438.1 6.1 all-gather.3.cloned.1.call-done
  444.2 229.0 %reduce-scatter.5.cloned.1.call-done = bf16[128,3456]{1,0:T(8,128)(2,1)} async-done(((bf16[2048,3456]{1,0:T(8,128)(2,1)}), bf16[128,3456]{1,0:T(8,128)(2,1)}) %reduce-scatter.5.cloned.1.call-update) | async-done | bytes 884752 | tf_op jit(solution)/shard_map/reduce_scatter | solution.py:46
  673.3 370.5 %all-gather.5.cloned.1.call-done = bf16[5120,3456]{1,0:T(8,128)(2,1)} async-done(((bf16[320,3456]{1,0:T(8,128)(2,1)}), bf16[5120,3456]{1,0:T(8,128)(2,1)}) %all-gather.5.cloned.1.call-update) | async-done | bytes 35389456 | tf_op jit(solution)/shard_map/all_gather | solution.py:85
  1043.8 8.3 fusion.4
  1052.1 7.8 convolution_add_fusion.5
  1059.9 8.0 convolution_add_fusion.4
  1067.9 7.8 fusion
  1075.7 7.8 fusion.5
  1083.5 8.1 convolution_add_fusion.2
  1091.5 8.5 convolution_add_fusion.1
  1100.1 8.0 fusion.1
  1108.0 0.1 fusion.8
  1108.2 0.1 multiply_reduce_fusion
  1108.2 2.5 psum.31
  1110.7 0.6 broadcast_multiply_fusion
  (29 shorter events, 0.2 us)
Async XLA Ops:
  6.5 42.5 %copy-start = (bf16[320,2560]{1,0:T(8,128)(2,1)S(1)}, bf16[320,2560]{1,0:T(8,128)(2,1)}, u32[]{:S(2)}) copy-start(bf16[320,2560]{1,0:T(8,128)(2,1)} %param.13) | copy-start | bytes 4915204
  6.5 310.8 %reduce-scatter.3.cloned.1.call-start = ((), (), s32[]{:S(2)}) async-start(), calls=%async_computation.6 | async-start | bytes 11141120 | tf_op jit(solution)/shard_map/reduce_scatter | solution.py:40
  57.3 0.7 copy-start.5
  57.3 6.3 copy-start.3
  60.1 19.6 %all-to-all-start = ((bf16[16,2,160]{2,1,0:T(2,128)(2,1)}), bf16[16,2,160]{2,1,0:T(2,128)(2,1)S(1)}, u32[]{:S(2)}, u32[]{:S(2)}) async-start(bf16[16,2,160]{2,1,0:T(2,128)(2,1)} %reshape.42), calls=%async_computation | async-start | bytes 32768 | tf_op jit(solution)/shard_map/all_to_all | solution.py:33
  79.7 11.4 %all-to-all-start.3 = ((bf16[16,2,432]{2,1,0:T(2,128)(2,1)}), bf16[16,2,432]{2,1,0:T(2,128)(2,1)S(1)}, u32[]{:S(2)}, u32[]{:S(2)}) async-start(bf16[16,2,432]{2,1,0:T(2,128)(2,1)} %reshape.44), calls=%async_computation.5 | async-start | bytes 65536 | tf_op jit(solution)/shard_map/all_to_all | solution.py:35
  91.1 226.8 %all-to-all-start.2 = ((bf16[128,16,864]{0,2,1:T(8,128)(2,1)}), bf16[128,16,864]{0,2,1:T(8,128)(2,1)}, u32[]{:S(2)}, u32[]{:S(2)}) async-start(bf16[128,16,864]{0,2,1:T(8,128)(2,1)} %bitcast.37), calls=%async_computation.3 | async-start | bytes 7077888 | tf_op jit(solution)/shard_map/all_to_all | solution.py:34
  96.0 338.0 %all-reduce.3.cloned.1.call-start = ((), (), s32[]{:S(2)}) async-start(), calls=%async_computation.10 | async-start | bytes 385024 | tf_op jit(solution)/shard_map/psum | solution.py:57
  101.5 342.7 %all-gather.3.cloned.1.call-start = ((), (), s32[]{:S(2)}) async-start(), calls=%async_computation.7 | async-start | bytes 1966080 | tf_op jit(solution)/shard_map/all_gather | solution.py:75
  317.4 355.9 %reduce-scatter.5.cloned.1.call-start = ((), (), s32[]{:S(2)}) async-start(), calls=%async_computation.8 | async-start | bytes 15040512 | tf_op jit(solution)/shard_map/reduce_scatter | solution.py:46
  339.6 46.1 %copy-start.8 = (s32[128]{0:T(128)S(1)}, s32[128]{0:T(128)}, u32[]{:S(2)}) copy-start(s32[128]{0:T(128)} %param.16) | copy-start | bytes 1540
  339.6 704.1 %all-gather.5.cloned.1.call-start = ((), (), s32[]{:S(2)}) async-start(), calls=%async_computation.9 | async-start | bytes 37601280 | tf_op jit(solution)/shard_map/all_gather | solution.py:85
  1043.8 8.3 copy-start.6
  1043.8 8.3 copy-start.7
  1100.0 8.0 copy-start.2
  1100.1 8.1 copy-start.4
  1100.1 11.2 %copy-start.1 = (bf16[320,2560]{1,0:T(8,128)(2,1)S(1)}, bf16[320,2560]{1,0:T(8,128)(2,1)}, u32[]{:S(2)}) copy-start(bf16[320,2560]{1,0:T(8,128)(2,1)} %param.13) | copy-start | bytes 4915204
Sparse Core Ops, SparseCore 0:
  57.4 259.8 reduce-scatter.2
  322.7 111.3 all-reduce.2
  435.7 8.4 all-gather.2
  450.8 222.3 reduce-scatter.4
  675.9 367.8 all-gather.4
where the time goes:
time: 1120 us
  waiting for transfers between devices  887 us (79%)
  matrix products  99.3 us (9%)
  blocking collectives  89.7 us (8%)
  between operations  14.4 us (1%)
  starting transfers between devices  12.5 us (1%)
    all_gather x1, waiting for transfers between devices, body(): piece = lax.all_gather(corrected, 'seq', axis=0, tiled=True)  370 us
    reduce_scatter x1, waiting for transfers between devices, body(): lax.psum_scatter(jnp.dot(block_out, output_basis, preferred_element_type=...  229 us
    reduce_scatter x1, waiting for transfers between devices, body(): lax.psum_scatter(jnp.dot(block_in, input_basis, preferred_element_type=jn...  216 us
    dot_general x8, matrix products, body(): jnp.dot(q_cols, scaled, preferred_element_type=jnp.float32)  64.2 us
    psum x1, waiting for transfers between devices, body(): lax.psum(jnp.dot(block_qin, input_basis, preferred_element_type=jnp.float...  48.3 us
    psum x1, blocking collectives, body(): lax.psum(placed.astype(jnp.bfloat16), 'seq').astype(jnp.float32)  44.2 us
    all_to_all x1, blocking collectives, body(): lax.all_to_all(train_in, 'seq', split_axis=1, concat_axis=0, tiled=True)  40.6 us
  transfers between devices with their start and end apart: 8, of which 7 were waited for; matrix products, arithmetic and copies ran while one was open for 3% of the time, Pallas kernels for 0%

commit v1 on v0

v1 whole, which is shorter than its diff:
```python
import functools
import math

import jax
import jax.numpy as jnp
from jax import lax
from jax.experimental import pallas as pl
from jax.experimental.pallas import tpu as pltpu
from jax.sharding import PartitionSpec as P

DIN = 5120
EIGOUT = 6912
TOK_DEV = 128
SEQ_DEV = 2
QUERIES = 16
DAMPING = 0.1
INNER = 4
F32 = jnp.float32
BF16 = jnp.bfloat16
NT = (((1,), (1,)), ((), ()))
VMEM = pl.BlockSpec(memory_space=pltpu.VMEM)
SMEM = pl.BlockSpec(memory_space=pltpu.SMEM)


def bits(count):
    return range(count.bit_length() - 1)


def pick(x, index, axis=0):
    return lax.dynamic_index_in_dim(x, index, axis, keepdims=False)


def swap(x, axis, mask):
    size = lax.axis_size(axis)
    return lax.ppermute(x, axis, [(i, i ^ mask) for i in range(size)])


def unxor(x, index):
    size = x.shape[0]
    for b in bits(size):
        pairs = x.reshape((size >> (b + 1), 2, 1 << b) + x.shape[1:])
        turned = jnp.concatenate([pairs[:, 1:], pairs[:, :1]], axis=1)
        x = jnp.where((index >> b) & 1 == 1, turned, pairs).reshape(x.shape)
    return x


def add(*terms):
    total = terms[0].astype(F32)
    for term in terms[1:]:
        total = total + term.astype(F32)
    return total.astype(BF16)


def group_rows(parts, e, index):
    shares = []
    for h in range(len(parts)):
        share = parts[0][index]
        for m in range(1, len(parts)):
            share = jnp.where((e ^ m) == h, parts[m][index], share)
        shares.append(share)
    return jnp.concatenate(shares, axis=0) if len(shares) > 1 else shares[0]


def rotate_in_kernel(n, blocks, position, *refs):
    where, query, basis, parts, out = refs[0], refs[1], refs[2], refs[3:-1], refs[-1]
    me, e = where[0], where[1]
    width = basis.shape[0] // blocks

    def store(group, product, lane):
        for k in range(blocks):
            out[k, group] = product[
                k * width : (k + 1) * width, lane * TOK_DEV : (lane + 1) * TOK_DEV
            ].astype(BF16)

    store(n, lax.dot_general(basis[...], query[...], NT, preferred_element_type=F32), 0)

    @pl.loop(0, n // 4)
    def _(step):
        rows = [group_rows(parts, e, position((step * 4 + p) ^ me)) for p in range(4)]
        product = lax.dot_general(
            basis[...], jnp.concatenate(rows, axis=0), NT, preferred_element_type=F32
        )
        for p in range(4):
            store(step * 4 + p, product, p)


def rotate_in(where, query, basis, parts, n, blocks, position):
    width = basis.shape[0] // blocks
    return pl.pallas_call(
        functools.partial(rotate_in_kernel, n, blocks, position),
        out_shape=jax.ShapeDtypeStruct((blocks, n + 1, width, TOK_DEV), BF16),
        in_specs=[SMEM] + [VMEM] * (2 + len(parts)),
        out_specs=VMEM,
        compiler_params=pltpu.CompilerParams(vmem_limit_bytes=40 << 20),
        cost_estimate=pl.CostEstimate(
            flops=2 * (n + 1) * TOK_DEV * basis.size,
            bytes_accessed=2 * (basis.size + 2 * n * TOK_DEV * basis.shape[1]),
            transcendentals=0,
        ),
    )(where, query, basis, *parts)


def rotate_out_kernel(chunk, outer, where, basis, *refs):
    parts, (sx, kx, sy, ky) = refs[:-4], refs[-4:]
    me, e = where[0], where[1]
    half = outer // 2
    rows = [group_rows(parts, e, (chunk * outer + p) ^ me) for p in range(outer)]
    product = lax.dot_general(
        basis[0], jnp.concatenate(rows, axis=0), NT, preferred_element_type=F32
    )
    low = [product[:, p * TOK_DEV : (p + 1) * TOK_DEV].astype(BF16) for p in range(half)]
    high = [
        product[:, p * TOK_DEV : (p + 1) * TOK_DEV].astype(BF16) for p in range(half, outer)
    ]

    def put(ref, place, values):
        for p, value in enumerate(values):
            ref[place, p] = value

    for r, (a, i, b, j) in enumerate(
        [(kx, 0, ky, 0), (sx, 0, ky, 1), (kx, 1, sy, 0), (sx, 1, sy, 1)]
    ):

        @pl.when(pl.program_id(0) == r)
        def _(a=a, i=i, b=b, j=j):
            put(a, i, low)
            put(b, j, high)


def rotate_out(where, basis, parts, chunk, outer):
    _, cols, depth = basis.shape
    half = outer // 2
    whole = jax.ShapeDtypeStruct((2, half, cols, TOK_DEV), BF16)
    kept = pl.BlockSpec(whole.shape, lambda r, w: (0, 0, 0, 0))
    return pl.pallas_call(
        functools.partial(rotate_out_kernel, chunk, outer),
        out_shape=[whole] * 4,
        grid_spec=pltpu.PrefetchScalarGridSpec(
            num_scalar_prefetch=1,
            grid=(INNER,),
            in_specs=[pl.BlockSpec((1, cols, depth), lambda r, w: (r ^ (w[0] % INNER), 0, 0))]
            + [pl.BlockSpec(part.shape, lambda r, w: (0, 0, 0)) for part in parts],
            out_specs=[kept] * 4,
        ),
        compiler_params=pltpu.CompilerParams(vmem_limit_bytes=40 << 20),
        cost_estimate=pl.CostEstimate(
            flops=2 * outer * TOK_DEV * basis.size,
            bytes_accessed=2 * (basis.size + outer * TOK_DEV * (INNER * cols + depth)),
            transcendentals=0,
        ),
    )(where, basis, *parts)


def score_kernel(chunk, outer, masks, where, b_ref, a_ref, inverse, query_b, seq, out):
    z = where[0] // INNER
    count, rows = a_ref.shape[0] - 1, a_ref.shape[1]
    tile = 256 if rows % 256 == 0 else 128
    for p, mask in enumerate(masks):
        place = z ^ mask
        group = chunk * outer + place
        for member in range(SEQ_DEV):
            b = jnp.where(seq[group] == member, b_ref[p].astype(F32), 0.0).astype(BF16)
            total = jnp.zeros((b.shape[0], TOK_DEV), F32)
            for start in range(0, rows, tile):
                grad = lax.dot_general(
                    b, a_ref[group, start : start + tile], NT, preferred_element_type=F32
                )
                scaled = (grad * inverse[:, start : start + tile]).astype(BF16)
                total = total + jnp.dot(
                    scaled, a_ref[count, start : start + tile], preferred_element_type=F32
                )
            out[place, member : member + 1] = jnp.sum(
                total * query_b[...], axis=0, keepdims=True
            )


def score(where, b, a, inverse, query_b, seq, chunk, outer, masks):
    cols, rows = inverse.shape
    return pl.pallas_call(
        functools.partial(score_kernel, chunk, outer, masks),
        out_shape=jax.ShapeDtypeStruct((outer, SEQ_DEV, TOK_DEV), F32),
        in_specs=[SMEM] + [VMEM] * 5,
        out_specs=VMEM,
        compiler_params=pltpu.CompilerParams(vmem_limit_bytes=48 << 20),
        cost_estimate=pl.CostEstimate(
            flops=8 * outer * SEQ_DEV * TOK_DEV * cols * rows,
            bytes_accessed=2 * (b.size + a.size + 2 * inverse.size),
            transcendentals=0,
        ),
    )(where, b, a, inverse, query_b, seq)


def body(
    train_in,
    train_out,
    query_in,
    query_out,
    input_basis,
    output_basis,
    corrected,
    train_seq,
    query_order,
):
    n, size = lax.axis_size("seq"), lax.axis_size("eig")
    outer = n // INNER
    me, e = lax.axis_index("seq"), lax.axis_index("eig")
    xy, z = me % INNER, me // INNER
    where = jnp.stack([me, e]).astype(jnp.int32)
    share = TOK_DEV // size
    query_rows = query_in.shape[0]
    depth_out, cols = output_basis.shape
    cols_own = cols // INNER
    rows_own = corrected.shape[0]
    rows_in = rows_own * INNER
    per_core = input_basis.shape[1] // rows_in

    own = lax.dynamic_slice_in_dim(train_out, e * share, share, 0)
    own = own.reshape(share, n, depth_out).transpose(1, 0, 2)
    out_rel = jnp.stack(
        [pick(own, me)] + [swap(pick(own, me ^ m), "seq", m) for m in range(1, n)]
    )
    out_parts = [out_rel] + [swap(out_rel, "eig", m) for m in range(1, size)]

    small = jnp.concatenate(
        [
            query_in,
            query_out,
            train_seq.astype(BF16).reshape(query_rows, -1),
            (query_order % QUERIES).astype(BF16)[:, None],
        ],
        axis=1,
    )
    small = lax.all_gather(small, "seq", axis=0, tiled=True)
    din, dout = query_in.shape[1], query_out.shape[1]
    seq = small[:, din + dout : -1].reshape(n, 1, TOK_DEV).astype(F32)
    labels = small[:, -1].astype(F32)
    hot = (labels[:, None] == jnp.arange(QUERIES, dtype=F32)[None, :]).astype(F32)
    queries = small.shape[0]

    blocks = input_basis.reshape(rows_own, per_core, INNER, rows_own).transpose(2, 0, 1, 3)
    blocks = blocks.reshape(INNER, rows_own, per_core * rows_own)
    basis_in = jnp.stack(
        [pick(blocks, xy)] + [swap(pick(blocks, xy ^ r), "seq", r) for r in range(1, INNER)]
    )
    basis_in = unxor(basis_in, xy).reshape(rows_in, -1).T

    own = lax.dynamic_slice_in_dim(train_in, e * share, share, 0)
    own = own.reshape(share, outer, rows_in).transpose(1, 0, 2)
    in_rel = jnp.stack(
        [pick(own, z)]
        + [swap(pick(own, z ^ m), "seq", m * INNER) for m in range(1, outer)]
    )
    in_rel = jnp.concatenate([in_rel] + [swap(in_rel, "seq", r) for r in range(1, INNER)])
    in_parts = [in_rel] + [swap(in_rel, "eig", m) for m in range(1, size)]
    query_rows_in = lax.dynamic_slice_in_dim(small, z * rows_in, rows_in, 1)
    query_rows_in = jnp.pad(query_rows_in, ((0, TOK_DEV - queries), (0, 0)))
    rotated = rotate_in(
        where,
        query_rows_in,
        basis_in,
        in_parts,
        n,
        per_core,
        lambda rel: (rel % INNER) * outer + rel // INNER,
    )
    rotated = rotated.reshape(per_core, n + 1, size, rows_own // size, TOK_DEV)
    rotated = jnp.stack(
        [pick(rotated, e, 2)]
        + [swap(pick(rotated, e ^ m, 2), "eig", m) for m in range(1, size)]
    )
    rotated = unxor(rotated, e).reshape((outer,) + rotated.shape[2:])
    for b in bits(outer):
        bit = (z >> b) & 1
        pairs = rotated.reshape((-1, 2) + rotated.shape[1:])
        rotated = add(
            pick(pairs, bit, 1), swap(pick(pairs, 1 - bit, 1), "seq", INNER << b)
        )
    rotated = rotated[0]
    rotated = jnp.stack([rotated] + [swap(rotated, "seq", r) for r in range(1, INNER)])
    rotated = jnp.stack([rotated] + [swap(rotated, "eig", m) for m in range(1, size)])
    full_a = unxor(rotated, e).transpose(2, 1, 0, 3, 4).reshape(n + 1, rows_in, TOK_DEV)

    blocks = corrected.reshape(rows_own, INNER, cols_own).transpose(1, 0, 2)
    piece = jnp.concatenate(
        [pick(blocks, xy)] + [swap(pick(blocks, xy ^ r), "seq", r) for r in range(1, INNER)]
    )
    inverse = 1.0 / (piece.T.astype(F32) + DAMPING)

    query_b = lax.dynamic_slice_in_dim(small, din + me * depth_out, depth_out, 1)
    query_b = jnp.dot(query_b, output_basis, preferred_element_type=F32).astype(BF16)
    for b in bits(n):
        query_b = add(query_b, swap(query_b, "seq", 1 << b))
    query_b = lax.dynamic_slice_in_dim(query_b, xy * cols_own, cols_own, 1)
    query_b = jnp.pad(query_b.astype(F32), ((0, TOK_DEV - queries), (0, 0))).T

    basis_out = output_basis.reshape(depth_out, INNER, cols_own).transpose(1, 2, 0)
    found = []
    for chunk in range(INNER):
        sx, kx, sy, ky = rotate_out(where, basis_out, out_parts, chunk, outer)
        rx, ry = swap(sx, "seq", 1), swap(sy, "seq", 2)
        low = add(kx[0], rx[0], swap(add(kx[1], rx[1]), "seq", 2))
        high = add(ky[0], ry[0], swap(add(ky[1], ry[1]), "seq", 1))
        held = jnp.concatenate([low, high])
        for b in bits(outer):
            bit = (z >> b) & 1
            pairs = held.reshape((-1, 2) + held.shape[1:])
            held = add(
                pick(pairs, bit, 1), swap(pick(pairs, 1 - bit, 1), "seq", INNER << b)
            )
        masks = [0]
        for b in reversed(bits(outer)):
            held = jnp.concatenate([held, swap(held, "seq", INNER << b)])
            masks = masks + [m | (1 << b) for m in masks]
        found.append(
            score(where, held, full_a, inverse, query_b, seq, chunk, outer, masks)
        )
    per_token = jnp.concatenate(found)[:, :, :queries]
    scores = jnp.sum(per_token[:, :, :, None] * hot[None, None], axis=2)
    scores = lax.all_to_all(scores, "seq", split_axis=0, concat_axis=0, tiled=True)
    scores = jnp.sum(scores, axis=0)
    for b in bits(size):
        scores = scores + swap(scores, "eig", 1 << b)
    factor = 1.0 / math.sqrt(DIN * EIGOUT * (TOK_DEV / SEQ_DEV) * (queries / QUERIES))
    return scores * factor


def solution(mesh):
    placed = (
        P("seq", None),
        P("seq", None),
        P("seq", None),
        P("seq", None),
        P("seq", "eig"),
        P("seq", "eig"),
        P("seq", "eig"),
        P("seq"),
        P("seq"),
    )
    return jax.shard_map(
        body, mesh=mesh, in_specs=placed, out_specs=P("seq", None), check_vma=False
    )
```

time: 1120 us -> 703 us (0.63)
  waiting for transfers between devices: 887 us -> 267 us
  local copies, waits for them, and re-layouts: 11 us -> 137 us
  matrix products: 99.3 us -> 4.24 us
  Pallas kernels: 0 us -> 90.2 us
  starting transfers between devices: 12.5 us -> 87.3 us
  other arithmetic: 4.75 us -> 48.4 us
  blocking collectives: 89.7 us -> 62 us
  between operations: 14.4 us -> 1.95 us
    reduce_scatter x2 -> x0, waiting for transfers between devices: 445 us -> none  [the longest x1 229 us: body(): lax.psum_scatter(jnp.dot(block_out, output_basis, preferred_element_type=...]
    all_gather x2 -> x0, waiting for transfers between devices: 377 us -> none  [the longest x1 370 us: body(): piece = lax.all_gather(corrected, 'seq', axis=0, tiled=True)]
    ppermute x0 -> x73, waiting for transfers between devices: none -> 267 us  [swap(): return lax.ppermute(x, axis, [(i, i ^ mask) for i in range(size)])]
    dot_general x12 -> x1, matrix products: 99.3 us -> 4.24 us  [body(): jnp.dot(query_b, output_basis, preferred_element_type=F32).astype(BF16)]
    pallas_call x0 -> x9, Pallas kernels: none -> 90.2 us  [the longest x4 50.4 us: score(): pl.pallas_call(functools.partial(score_kernel, chunk, outer, masks), out_...]
    ppermute x0 -> x73, starting transfers between devices: none -> 87.3 us  [swap(): return lax.ppermute(x, axis, [(i, i ^ mask) for i in range(size)])]
    all_gather x1, blocking collectives: 2.41 us -> 51.4 us  [body(): small = lax.all_gather(small, 'seq', axis=0, tiled=True)]
    psum x1 -> x0, waiting for transfers between devices: 48.3 us -> none  [body(): lax.psum(jnp.dot(block_qin, input_basis, preferred_element_type=jnp.float...]
  transfers between devices with their start and end apart: 8 -> 73, of which waited for: 7 -> 36; matrix products, arithmetic and copies ran while one was open for 3% -> 23% of each run, Pallas kernels for 0% -> 6%
where the time goes in v1:
time: 703 us; the launch traced here: 698 us
  waiting for transfers between devices  267 us (38%)
  local copies, waits for them, and re-layouts  137 us (19%)
  Pallas kernels  90.2 us (13%)
  starting transfers between devices  87.3 us (12%)
  blocking collectives  62 us (9%)
  other arithmetic  48.4 us (7%)
    ppermute x73, waiting for transfers between devices, swap(): return lax.ppermute(x, axis, [(i, i ^ mask) for i in range(size)])  267 us
    ppermute x73, starting transfers between devices, swap(): return lax.ppermute(x, axis, [(i, i ^ mask) for i in range(size)])  87.3 us
    unnamed x125, local copies, waits for them, and re-layouts  58 us
    all_gather x1, blocking collectives, body(): small = lax.all_gather(small, 'seq', axis=0, tiled=True)  51.4 us
    pallas_call x4, Pallas kernels, score(): pl.pallas_call(functools.partial(score_kernel, chunk, outer, masks), out_...  50.4 us
    pallas_call x4, Pallas kernels, rotate_out(): pl.pallas_call(functools.partial(rotate_out_kernel, chunk, outer), out_sh...  33.2 us
    convert_element_type x30, other arithmetic, add(): return total.astype(BF16)  24.6 us
  transfers between devices with their start and end apart: 73, of which 36 were waited for; matrix products, arithmetic and copies ran while one was open for 23% of the time, Pallas kernels for 6%

profile of v1, /device:TPU:0, one launch (start us, length us, event | category | flops | bytes accessed | tf_op | source)
XLA Modules:
  0.0 697.5 jit_solution(3472568507679472102)
XLA Ops:
  4.7 4.0 constant_dynamic-slice_fusion.10
  17.9 51.4 %all-gather = bf16[16,1,19073]{2,1,0:T(2,128)(2,1)} all-gather(bf16[1,1,19073]{2,1,0:T(2,128)(2,1)S(1)} %maximum_bitcast_fusion.1), channel_id=1, replica_groups=mesh['seq'=16,'eig'=2] {'seq'}, dimensions={0}, use_global_device_ids=true | all-gather | bytes 648482 | tf_op jit(solution)/shard_map/all_gather | solution.py:233
  70.3 4.2 convolution_convert_fusion
  75.9 4.6 reshape.375
  80.6 5.1 constant_dynamic-slice_fusion.18
  91.0 9.3 %copy.184 = bf16[864,3456]{0,1:T(8,128)(2,1)} copy(bf16[864,3456]{1,0:T(8,128)(2,1)} %param.14) | data formatting | bytes 11943936 | tf_op args[5]
  125.7 3.5 reshape.388
  131.9 4.9 constant_dynamic-slice_fusion.5
  165.1 5.5 collective-permute-done.6
  174.4 5.4 collective-permute-done.8
  215.5 7.5 %collective-permute-done.45 = bf16[16,3456]{1,0:T(8,128)(2,1)S(1)} collective-permute-done((bf16[16,3456]{1,0:T(8,128)(2,1)S(1)}, bf16[16,3456]{1,0:T(8,128)(2,1)S(1)}, u32[]{:S(2)}, u32[]{:S(2)}) %collective-permute-start.45) | collective-permute-done | bytes 110624 | tf_op jit(solution)/shard_map/ppermute | solution.py:35
  236.5 4.7 collective-permute-start.47
  251.0 3.7 copy.191
  256.0 3.6 copy.193
  272.8 5.1 concatenate.125
  280.0 14.2 %collective-permute-done.31 = bf16[4,64,1280]{2,1,0:T(8,128)(2,1)} collective-permute-done((bf16[4,64,1280]{2,1,0:T(8,128)(2,1)}, bf16[4,64,1280]{2,1,0:T(8,128)(2,1)}, u32[]{:S(2)}, u32[]{:S(2)}) %collective-permute-start.31) | collective-permute-done | bytes 655392 | tf_op jit(solution)/shard_map/ppermute | solution.py:35
  298.9 9.0 %shard_map.98 = (bf16[2,2,864,128]{3,2,1,0:T(8,128)(2,1)}, bf16[2,2,864,128]{3,2,1,0:T(8,128)(2,1)S(1)}, bf16[2,2,864,128]{3,2,1,0:T(8,128)(2,1)}, bf16[2,2,864,128]{3,2,1,0:T(8,128)(2,1)S(1)}) custom-call(s32[2]{0:T(128)S(1)} %pad_add_fusion.where.refs_0_, bf16[4,864,864]{2,1,0:T(8,128)(2,1)S(1)} %bitcast.276, ...), custom_call_target="tpu_custom_call" | custom-call | flops 3057647616 | bytes 10395648 | tf_op jit(solution)/shard_map/pallas_call | solution.py:135
  310.6 9.1 %shard_map.96 = (bf16[2,2,864,128]{3,2,1,0:T(8,128)(2,1)}, bf16[2,2,864,128]{3,2,1,0:T(8,128)(2,1)S(1)}, bf16[2,2,864,128]{3,2,1,0:T(8,128)(2,1)}, bf16[2,2,864,128]{3,2,1,0:T(8,128)(2,1)S(1)}) custom-call(s32[2]{0:T(128)S(1)} %pad_add_fusion.where.refs_0_, bf16[4,864,864]{2,1,0:T(8,128)(2,1)S(1)} %bitcast.277, ...), custom_call_target="tpu_custom_call" | custom-call | flops 3057647616 | bytes 10395648 | tf_op jit(solution)/shard_map/pallas_call | solution.py:135
  322.3 7.6 %shard_map.94 = (bf16[2,2,864,128]{3,2,1,0:T(8,128)(2,1)S(1)}, bf16[2,2,864,128]{3,2,1,0:T(8,128)(2,1)S(1)}, bf16[2,2,864,128]{3,2,1,0:T(8,128)(2,1)S(1)}, bf16[2,2,864,128]{3,2,1,0:T(8,128)(2,1)S(1)}) custom-call(s32[2]{0:T(128)S(1)} %pad_add_fusion.where.refs_0_, bf16[4,864,864]{2,1,0:T(8,128)(2,1)S(1)} %bitcast.278, ...), custom_call_target="tpu_custom_call" | custom-call | flops 3057647616 | bytes 10395648 | tf_op jit(solution)/shard_map/pallas_call | solution.py:135
  330.9 7.6 %shard_map.91 = (bf16[2,2,864,128]{3,2,1,0:T(8,128)(2,1)S(1)}, bf16[2,2,864,128]{3,2,1,0:T(8,128)(2,1)S(1)}, bf16[2,2,864,128]{3,2,1,0:T(8,128)(2,1)S(1)}, bf16[2,2,864,128]{3,2,1,0:T(8,128)(2,1)S(1)}) custom-call(s32[2]{0:T(128)S(1)} %pad_add_fusion.where.refs_0_, bf16[4,864,864]{2,1,0:T(8,128)(2,1)S(1)} %bitcast.279, ...), custom_call_target="tpu_custom_call" | custom-call | flops 3057647616 | bytes 10395648 | tf_op jit(solution)/shard_map/pallas_call | solution.py:135
  343.0 6.8 collective-permute-done.56
  355.0 13.7 %collective-permute-done.48 = bf16[2,2,864,128]{3,2,1,0:T(8,128)(2,1)S(1)} collective-permute-done((bf16[2,2,864,128]{3,2,1,0:T(8,128)(2,1)}, bf16[2,2,864,128]{3,2,1,0:T(8,128)(2,1)S(1)}, u32[]{:S(2)}, u32[]{:S(2)}) %collective-permute-start.48) | collective-permute-done | bytes 884768 | tf_op jit(solution)/shard_map/ppermute | solution.py:35
  372.8 14.8 %collective-permute-done.16 = bf16[2,2,864,128]{3,2,1,0:T(8,128)(2,1)S(1)} collective-permute-done((bf16[2,2,864,128]{3,2,1,0:T(8,128)(2,1)S(1)}, bf16[2,2,864,128]{3,2,1,0:T(8,128)(2,1)S(1)}, u32[]{:S(2)}, u32[]{:S(2)}) %collective-permute-start.16) | collective-permute-done | bytes 884768 | tf_op jit(solution)/shard_map/ppermute | solution.py:35
  391.7 6.8 collective-permute-done.65
  401.8 6.6 shard_map.92
  423.1 3.4 collective-permute-done.17
  429.1 31.4 %collective-permute-done.35 = bf16[2,17,160,128]{3,2,1,0:T(8,128)(2,1)S(1)} collective-permute-done((bf16[2,17,160,128]{3,2,1,0:T(8,128)(2,1)S(1)}, bf16[2,17,160,128]{3,2,1,0:T(8,128)(2,1)S(1)}, u32[]{:S(2)}, u32[]{:S(2)}) %collective-permute-start.35) | collective-permute-done | bytes 1392672 | tf_op jit(solution)/shard_map/ppermute | solution.py:35
  464.2 25.5 %collective-permute-done.60 = bf16[2,864,128]{2,1,0:T(8,128)(2,1)S(1)} collective-permute-done((bf16[2,864,128]{2,1,0:T(8,128)(2,1)S(1)}, bf16[2,864,128]{2,1,0:T(8,128)(2,1)S(1)}, u32[]{:S(2)}, u32[]{:S(2)}) %collective-permute-start.60) | collective-permute-done | bytes 442400 | tf_op jit(solution)/shard_map/ppermute | solution.py:35
  489.9 11.6 %collective-permute-done.36 = bf16[1,17,160,128]{3,2,1,0:T(8,128)(2,1)S(1)} collective-permute-done((bf16[1,17,160,128]{3,2,1,0:T(8,128)(2,1)S(1)}, bf16[1,17,160,128]{3,2,1,0:T(8,128)(2,1)S(1)}, u32[]{:S(2)}, u32[]{:S(2)}) %collective-permute-start.36) | collective-permute-done | bytes 696352 | tf_op jit(solution)/shard_map/ppermute | solution.py:35
  509.0 12.2 %collective-permute-done.39 = bf16[17,160,128]{2,1,0:T(8,128)(2,1)S(1)} collective-permute-done((bf16[17,160,128]{2,1,0:T(8,128)(2,1)S(1)}, bf16[17,160,128]{2,1,0:T(8,128)(2,1)S(1)}, u32[]{:S(2)}, u32[]{:S(2)}) %collective-permute-start.39) | collective-permute-done | bytes 696352 | tf_op jit(solution)/shard_map/ppermute | solution.py:35
  521.2 3.4 collective-permute-start.53
  524.5 7.5 %collective-permute-done.38 = bf16[17,160,128]{2,1,0:T(8,128)(2,1)S(1)} collective-permute-done((bf16[17,160,128]{2,1,0:T(8,128)(2,1)S(1)}, bf16[17,160,128]{2,1,0:T(8,128)(2,1)S(1)}, u32[]{:S(2)}, u32[]{:S(2)}) %collective-permute-start.38) | collective-permute-done | bytes 696352 | tf_op jit(solution)/shard_map/ppermute | solution.py:35
  532.1 3.4 collective-permute-start.21
  539.4 21.3 %collective-permute-done.21 = bf16[1,864,128]{2,1,0:T(8,128)(2,1)S(1)} collective-permute-done((bf16[1,864,128]{2,1,0:T(8,128)(2,1)S(1)}, bf16[1,864,128]{2,1,0:T(8,128)(2,1)S(1)}, u32[]{:S(2)}, u32[]{:S(2)}) %collective-permute-start.21) | collective-permute-done | bytes 221216 | tf_op jit(solution)/shard_map/ppermute | solution.py:35
  560.8 9.3 %collective-permute-done.70 = bf16[1,864,128]{2,1,0:T(8,128)(2,1)S(1)} collective-permute-done((bf16[1,864,128]{2,1,0:T(8,128)(2,1)S(1)}, bf16[1,864,128]{2,1,0:T(8,128)(2,1)S(1)}, u32[]{:S(2)}, u32[]{:S(2)}) %collective-permute-start.70) | collective-permute-done | bytes 221216 | tf_op jit(solution)/shard_map/ppermute | solution.py:35
  570.2 4.7 collective-permute-done.62
  575.1 4.6 collective-permute-done.54
  579.8 4.0 collective-permute-done.22
  584.5 8.7 %collective-permute-done.71 = bf16[2,864,128]{2,1,0:T(8,128)(2,1)S(1)} collective-permute-done((bf16[2,864,128]{2,1,0:T(8,128)(2,1)S(1)}, bf16[2,864,128]{2,1,0:T(8,128)(2,1)S(1)}, u32[]{:S(2)}, u32[]{:S(2)}) %collective-permute-start.71) | collective-permute-done | bytes 442400 | tf_op jit(solution)/shard_map/ppermute | solution.py:35
  593.4 9.4 %collective-permute-done.63 = bf16[2,864,128]{2,1,0:T(8,128)(2,1)S(1)} collective-permute-done((bf16[2,864,128]{2,1,0:T(8,128)(2,1)S(1)}, bf16[2,864,128]{2,1,0:T(8,128)(2,1)S(1)}, u32[]{:S(2)}, u32[]{:S(2)}) %collective-permute-start.63) | collective-permute-done | bytes 442400 | tf_op jit(solution)/shard_map/ppermute | solution.py:35
  602.9 9.4 %collective-permute-done.55 = bf16[2,864,128]{2,1,0:T(8,128)(2,1)S(1)} collective-permute-done((bf16[2,864,128]{2,1,0:T(8,128)(2,1)S(1)}, bf16[2,864,128]{2,1,0:T(8,128)(2,1)S(1)}, u32[]{:S(2)}, u32[]{:S(2)}) %collective-permute-start.55) | collective-permute-done | bytes 442400 | tf_op jit(solution)/shard_map/ppermute | solution.py:35
  612.3 9.3 %collective-permute-done.23 = bf16[2,864,128]{2,1,0:T(8,128)(2,1)S(1)} collective-permute-done((bf16[2,864,128]{2,1,0:T(8,128)(2,1)S(1)}, bf16[2,864,128]{2,1,0:T(8,128)(2,1)S(1)}, u32[]{:S(2)}, u32[]{:S(2)}) %collective-permute-start.23) | collective-permute-done | bytes 442400 | tf_op jit(solution)/shard_map/ppermute | solution.py:35
  625.7 6.2 copy_select_fusion
  631.9 12.4 %shard_map.99 = f32[4,2,128]{2,1,0:T(2,128)S(1)} custom-call(s32[2]{0:T(128)S(1)} %pad_add_fusion.where.refs_0_, bf16[4,864,128]{2,1,0:T(8,128)(2,1)S(1)} %pad_maximum_fusion.14.b_ref, bf16[17,1280,128]{2,1,0:T(8,128)(2,1)} %bitcast.291, f32[864,1280]{1,0:T(8,128)S(1)} %divide_bitcast_fusion.inverse, f32[864,128]{1,0:T(8,128)S(1)} %convert_bitcast_fusion.query_b, ...), custom_call_target="tpu_custom_call" | custom-call | flops 9059696640 | bytes 10878976 | tf_op jit(solution)/shard_map/pallas_call | solution.py:179
  644.3 12.8 %shard_map.97 = f32[4,2,128]{2,1,0:T(2,128)S(1)} custom-call(s32[2]{0:T(128)S(1)} %pad_add_fusion.where.refs_0_, bf16[4,864,128]{2,1,0:T(8,128)(2,1)S(1)} %pad_maximum_fusion.12.b_ref, bf16[17,1280,128]{2,1,0:T(8,128)(2,1)} %bitcast.292, f32[864,1280]{1,0:T(8,128)S(1)} %divide_bitcast_fusion.inverse, f32[864,128]{1,0:T(8,128)S(1)} %convert_bitcast_fusion.query_b, ...), custom_call_target="tpu_custom_call" | custom-call | flops 9059696640 | bytes 10878976 | tf_op jit(solution)/shard_map/pallas_call | solution.py:179
  657.2 12.6 %shard_map.95 = f32[4,2,128]{2,1,0:T(2,128)S(1)} custom-call(s32[2]{0:T(128)S(1)} %pad_add_fusion.where.refs_0_, bf16[4,864,128]{2,1,0:T(8,128)(2,1)S(1)} %pad_maximum_fusion.10.b_ref, bf16[17,1280,128]{2,1,0:T(8,128)(2,1)} %bitcast.293, f32[864,1280]{1,0:T(8,128)S(1)} %divide_bitcast_fusion.inverse, f32[864,128]{1,0:T(8,128)S(1)} %convert_bitcast_fusion.query_b, ...), custom_call_target="tpu_custom_call" | custom-call | flops 9059696640 | bytes 10878976 | tf_op jit(solution)/shard_map/pallas_call | solution.py:179
  670.8 12.6 %shard_map.93 = f32[4,2,128]{2,1,0:T(2,128)S(1)} custom-call(s32[2]{0:T(128)S(1)} %pad_add_fusion.where.refs_0_, bf16[4,864,128]{2,1,0:T(8,128)(2,1)S(1)} %pad_maximum_fusion.8.b_ref, bf16[17,1280,128]{2,1,0:T(8,128)(2,1)} %bitcast.294, f32[864,1280]{1,0:T(8,128)S(1)} %divide_bitcast_fusion.inverse, f32[864,128]{1,0:T(8,128)S(1)} %copy-done.4, ...), custom_call_target="tpu_custom_call" | custom-call | flops 9059696640 | bytes 10878976 | tf_op jit(solution)/shard_map/pallas_call | solution.py:179
  683.5 10.6 %all_to_all.5 = f32[16,2,16]{2,1,0:T(2,128)S(1)} all-to-all(f32[16,2,16]{2,1,0:T(2,128)S(1)} %multiply_reduce_fusion), channel_id=1, replica_groups=mesh['seq'=16,'eig'=2] {'seq'}, dimensions={0} | all-to-all | bytes 4096 | tf_op jit(solution)/shard_map/all_to_all | solution.py:319
  (349 shorter events, 230.4 us)
Async XLA Ops:
  9.3 197.4 %collective-permute-start.27 = (bf16[64,1280]{1,0:T(8,128)(2,1)}, bf16[64,1280]{1,0:T(8,128)(2,1)}, u32[]{:S(2)}, u32[]{:S(2)}) collective-permute-start(bf16[64,1280]{1,0:T(8,128)(2,1)} %bitcast.259), channel_id=1, source_target_pairs={{0,8},{2,10},{4,12},{6,14},{8,0},{10,2},{12,4},{14,6},{16,24},{18,... | collective-permute-start | bytes 491528 | tf_op jit(solution)/shard_map/ppermute | solution.py:35
  13.0 197.3 %collective-permute-start.28 = (bf16[64,1280]{1,0:T(8,128)(2,1)}, bf16[64,1280]{1,0:T(8,128)(2,1)}, u32[]{:S(2)}, u32[]{:S(2)}) collective-permute-start(bf16[64,1280]{1,0:T(8,128)(2,1)} %bitcast.258), channel_id=1, source_target_pairs={{0,16},{2,18},{4,20},{6,22},{8,24},{10,26},{12,28},{14,30},{16,0},... | collective-permute-start | bytes 491528 | tf_op jit(solution)/shard_map/ppermute | solution.py:35
  16.3 196.0 %collective-permute-start.29 = (bf16[64,1280]{1,0:T(8,128)(2,1)}, bf16[64,1280]{1,0:T(8,128)(2,1)}, u32[]{:S(2)}, u32[]{:S(2)}) collective-permute-start(bf16[64,1280]{1,0:T(8,128)(2,1)} %bitcast.257), channel_id=1, source_target_pairs={{0,24},{2,26},{4,28},{6,30},{8,16},{10,18},{12,20},{14,22},{16,8},... | collective-permute-start | bytes 491528 | tf_op jit(solution)/shard_map/ppermute | solution.py:35
  74.6 68.1 %collective-permute-start.44 = (bf16[16,3456]{1,0:T(8,128)(2,1)}, bf16[16,3456]{1,0:T(8,128)(2,1)}, u32[]{:S(2)}, u32[]{:S(2)}) collective-permute-start(bf16[16,3456]{1,0:T(8,128)(2,1)} %convolution_convert_fusion), channel_id=1, source_target_pairs={{0,2},{2,0},{4,6},{6,4},{8,10},{10,8},{12,14},{14,12},{16,18},{18,... | collective-permute-start | bytes 331784 | tf_op jit(solution)/shard_map/ppermute | solution.py:35
  86.4 61.2 %collective-permute-start = (bf16[64,864]{1,0:T(8,128)(2,1)}, bf16[64,864]{1,0:T(8,128)(2,1)}, u32[]{:S(2)}, u32[]{:S(2)}) collective-permute-start(bf16[64,864]{1,0:T(8,128)(2,1)} %bitcast.274), channel_id=1, source_target_pairs={{0,2},{2,0},{4,6},{6,4},{8,10},{10,8},{12,14},{14,12},{16,18},{18,... | collective-permute-start | bytes 331784 | tf_op jit(solution)/shard_map/ppermute | solution.py:35
  200.4 35.7 %collective-permute-start.26 = (bf16[320,640]{1,0:T(8,128)(2,1)}, bf16[320,640]{1,0:T(8,128)(2,1)}, u32[]{:S(2)}, u32[]{:S(2)}) collective-permute-start(bf16[320,640]{1,0:T(8,128)(2,1)} %get-tuple-element.77), channel_id=1, source_target_pairs={{0,6},{2,4},{4,2},{6,0},{8,14},{10,12},{12,10},{14,8},{16,22},{18,... | collective-permute-start | bytes 1228808 | tf_op jit(solution)/shard_map/ppermute | solution.py:35
  205.1 31.4 %collective-permute-start.25 = (bf16[320,640]{1,0:T(8,128)(2,1)}, bf16[320,640]{1,0:T(8,128)(2,1)}, u32[]{:S(2)}, u32[]{:S(2)}) collective-permute-start(bf16[320,640]{1,0:T(8,128)(2,1)} %get-tuple-element.78), channel_id=1, source_target_pairs={{0,4},{2,6},{4,0},{6,2},{8,12},{10,14},{12,8},{14,10},{16,20},{18,... | collective-permute-start | bytes 1228808 | tf_op jit(solution)/shard_map/ppermute | solution.py:35
  206.7 29.8 %collective-permute-start.24 = (bf16[320,640]{1,0:T(8,128)(2,1)}, bf16[320,640]{1,0:T(8,128)(2,1)}, u32[]{:S(2)}, u32[]{:S(2)}) collective-permute-start(bf16[320,640]{1,0:T(8,128)(2,1)} %get-tuple-element.79), channel_id=1, source_target_pairs={{0,2},{2,0},{4,6},{6,4},{8,10},{10,8},{12,14},{14,12},{16,18},{18,... | collective-permute-start | bytes 1228808 | tf_op jit(solution)/shard_map/ppermute | solution.py:35
  210.3 52.9 %collective-permute-start.42 = (bf16[320,864]{1,0:T(8,128)(2,1)}, bf16[320,864]{1,0:T(8,128)(2,1)}, u32[]{:S(2)}, u32[]{:S(2)}) collective-permute-start(bf16[320,864]{1,0:T(8,128)(2,1)} %bitcast.255), channel_id=1, source_target_pairs={{0,4},{2,6},{4,0},{6,2},{8,12},{10,14},{12,8},{14,10},{16,20},{18,... | collective-permute-start | bytes 1658888 | tf_op jit(solution)/shard_map/ppermute | solution.py:35
  232.4 34.7 %collective-permute-start.41 = (bf16[320,864]{1,0:T(8,128)(2,1)}, bf16[320,864]{1,0:T(8,128)(2,1)}, u32[]{:S(2)}, u32[]{:S(2)}) collective-permute-start(bf16[320,864]{1,0:T(8,128)(2,1)} %bitcast.256), channel_id=1, source_target_pairs={{0,2},{2,0},{4,6},{6,4},{8,10},{10,8},{12,14},{14,12},{16,18},{18,... | collective-permute-start | bytes 1658888 | tf_op jit(solution)/shard_map/ppermute | solution.py:35
  236.1 34.5 %collective-permute-start.43 = (bf16[320,864]{1,0:T(8,128)(2,1)}, bf16[320,864]{1,0:T(8,128)(2,1)}, u32[]{:S(2)}, u32[]{:S(2)}) collective-permute-start(bf16[320,864]{1,0:T(8,128)(2,1)} %bitcast.311), channel_id=1, source_target_pairs={{0,6},{2,4},{4,2},{6,0},{8,14},{10,12},{12,10},{14,8},{16,22},{18,... | collective-permute-start | bytes 1658888 | tf_op jit(solution)/shard_map/ppermute | solution.py:35
  236.5 59.6 %collective-permute-start.15 = (bf16[16,64,864]{2,1,0:T(8,128)(2,1)}, bf16[16,64,864]{2,1,0:T(8,128)(2,1)}, u32[]{:S(2)}, u32[]{:S(2)}) collective-permute-start(bf16[16,64,864]{2,1,0:T(8,128)(2,1)} %bitcast_dynamic-update-slice_fusion.1.refs_0_), channel_id=1, source_target_pairs={{0,1},{1,0},{2,3},{3,2},{4,5},{5,4},{6,7},{7,6},{8,9},{9,8},{10,11... | collective-permute-start | bytes 5308424 | tf_op jit(solution)/shard_map/ppermute | solution.py:35
  236.5 23.0 %collective-permute-start.47 = (bf16[16,3456]{1,0:T(8,128)(2,1)S(1)}, bf16[16,3456]{1,0:T(8,128)(2,1)S(1)}, u32[]{:S(2)}, u32[]{:S(2)}) collective-permute-start(bf16[16,3456]{1,0:T(8,128)(2,1)S(1)} %copy.215), channel_id=1, source_target_pairs={{0,16},{2,18},{4,20},{6,22},{8,24},{10,26},{12,28},{14,30},{16,0},... | collective-permute-start | bytes 331784 | tf_op jit(solution)/shard_map/ppermute | solution.py:35
  263.2 30.9 %collective-permute-start.31 = (bf16[4,64,1280]{2,1,0:T(8,128)(2,1)}, bf16[4,64,1280]{2,1,0:T(8,128)(2,1)}, u32[]{:S(2)}, u32[]{:S(2)}) collective-permute-start(bf16[4,64,1280]{2,1,0:T(8,128)(2,1)} %pad_maximum_fusion.15), channel_id=1, source_target_pairs={{0,4},{2,6},{4,0},{6,2},{8,12},{10,14},{12,8},{14,10},{16,20},{18,... | collective-permute-start | bytes 1966088 | tf_op jit(solution)/shard_map/ppermute | solution.py:35
  267.0 41.2 %collective-permute-start.32 = (bf16[4,64,1280]{2,1,0:T(8,128)(2,1)}, bf16[4,64,1280]{2,1,0:T(8,128)(2,1)}, u32[]{:S(2)}, u32[]{:S(2)}) collective-permute-start(bf16[4,64,1280]{2,1,0:T(8,128)(2,1)} %pad_maximum_fusion.15), channel_id=1, source_target_pairs={{0,6},{2,4},{4,2},{6,0},{8,14},{10,12},{12,10},{14,8},{16,22},{18,... | collective-permute-start | bytes 1966088 | tf_op jit(solution)/shard_map/ppermute | solution.py:35
  307.9 30.5 %collective-permute-start.64 = (bf16[2,2,864,128]{3,2,1,0:T(8,128)(2,1)}, bf16[2,2,864,128]{3,2,1,0:T(8,128)(2,1)}, u32[]{:S(2)}, u32[]{:S(2)}) collective-permute-start(bf16[2,2,864,128]{3,2,1,0:T(8,128)(2,1)} %get-tuple-element.34), channel_id=1, source_target_pairs={{0,2},{2,0},{4,6},{6,4},{8,10},{10,8},{12,14},{14,12},{16,18},{18,... | collective-permute-start | bytes 2654216 | tf_op jit(solution)/shard_map/ppermute | solution.py:35
  309.4 91.4 %collective-permute-start.33 = (bf16[16,64,1280]{2,1,0:T(8,128)(2,1)S(1)}, bf16[16,64,1280]{2,1,0:T(8,128)(2,1)}, u32[]{:S(2)}, u32[]{:S(2)}) collective-permute-start(bf16[16,64,1280]{2,1,0:T(8,128)(2,1)S(1)} %constant_dynamic-update-slice_fusion.refs_3_), channel_id=1, source_target_pairs={{0,1},{1,0},{2,3},{3,2},{4,5},{5,4},{6,7},{7,6},{8,9},{9,8},{10,11... | collective-permute-start | bytes 7864328 | tf_op jit(solution)/shard_map/ppermute | solution.py:35
  309.5 30.5 %collective-permute-start.66 = (bf16[2,2,864,128]{3,2,1,0:T(8,128)(2,1)}, bf16[2,2,864,128]{3,2,1,0:T(8,128)(2,1)}, u32[]{:S(2)}, u32[]{:S(2)}) collective-permute-start(bf16[2,2,864,128]{3,2,1,0:T(8,128)(2,1)} %get-tuple-element.36), channel_id=1, source_target_pairs={{0,4},{2,6},{4,0},{6,2},{8,12},{10,14},{12,8},{14,10},{16,20},{18,... | collective-permute-start | bytes 2654216 | tf_op jit(solution)/shard_map/ppermute | solution.py:35
  319.6 30.2 %collective-permute-start.56 = (bf16[2,2,864,128]{3,2,1,0:T(8,128)(2,1)}, bf16[2,2,864,128]{3,2,1,0:T(8,128)(2,1)}, u32[]{:S(2)}, u32[]{:S(2)}) collective-permute-start(bf16[2,2,864,128]{3,2,1,0:T(8,128)(2,1)} %get-tuple-element.30), channel_id=1, source_target_pairs={{0,2},{2,0},{4,6},{6,4},{8,10},{10,8},{12,14},{14,12},{16,18},{18,... | collective-permute-start | bytes 2654216 | tf_op jit(solution)/shard_map/ppermute | solution.py:35
  320.6 31.4 %collective-permute-start.58 = (bf16[2,2,864,128]{3,2,1,0:T(8,128)(2,1)}, bf16[2,2,864,128]{3,2,1,0:T(8,128)(2,1)}, u32[]{:S(2)}, u32[]{:S(2)}) collective-permute-start(bf16[2,2,864,128]{3,2,1,0:T(8,128)(2,1)} %get-tuple-element.32), channel_id=1, source_target_pairs={{0,4},{2,6},{4,0},{6,2},{8,12},{10,14},{12,8},{14,10},{16,20},{18,... | collective-permute-start | bytes 2654216 | tf_op jit(solution)/shard_map/ppermute | solution.py:35
  338.4 30.2 %collective-permute-start.48 = (bf16[2,2,864,128]{3,2,1,0:T(8,128)(2,1)}, bf16[2,2,864,128]{3,2,1,0:T(8,128)(2,1)S(1)}, u32[]{:S(2)}, u32[]{:S(2)}) collective-permute-start(bf16[2,2,864,128]{3,2,1,0:T(8,128)(2,1)} %copy-done.6), channel_id=1, source_target_pairs={{0,2},{2,0},{4,6},{6,4},{8,10},{10,8},{12,14},{14,12},{16,18},{18,... | collective-permute-start | bytes 2654216 | tf_op jit(solution)/shard_map/ppermute | solution.py:35
  339.9 30.2 %collective-permute-start.50 = (bf16[2,2,864,128]{3,2,1,0:T(8,128)(2,1)S(1)}, bf16[2,2,864,128]{3,2,1,0:T(8,128)(2,1)S(1)}, u32[]{:S(2)}, u32[]{:S(2)}) collective-permute-start(bf16[2,2,864,128]{3,2,1,0:T(8,128)(2,1)S(1)} %get-tuple-element.28), channel_id=1, source_target_pairs={{0,4},{2,6},{4,0},{6,2},{8,12},{10,14},{12,8},{14,10},{16,20},{18,... | collective-permute-start | bytes 2654216 | tf_op jit(solution)/shard_map/ppermute | solution.py:35
  349.8 37.8 %collective-permute-start.16 = (bf16[2,2,864,128]{3,2,1,0:T(8,128)(2,1)S(1)}, bf16[2,2,864,128]{3,2,1,0:T(8,128)(2,1)S(1)}, u32[]{:S(2)}, u32[]{:S(2)}) collective-permute-start(bf16[2,2,864,128]{3,2,1,0:T(8,128)(2,1)S(1)} %get-tuple-element.22), channel_id=1, source_target_pairs={{0,2},{2,0},{4,6},{6,4},{8,10},{10,8},{12,14},{14,12},{16,18},{18,... | collective-permute-start | bytes 2654216 | tf_op jit(solution)/shard_map/ppermute | solution.py:35
  352.0 37.1 %collective-permute-start.18 = (bf16[2,2,864,128]{3,2,1,0:T(8,128)(2,1)S(1)}, bf16[2,2,864,128]{3,2,1,0:T(8,128)(2,1)S(1)}, u32[]{:S(2)}, u32[]{:S(2)}) collective-permute-start(bf16[2,2,864,128]{3,2,1,0:T(8,128)(2,1)S(1)} %get-tuple-element.24), channel_id=1, source_target_pairs={{0,4},{2,6},{4,0},{6,2},{8,12},{10,14},{12,8},{14,10},{16,20},{18,... | collective-permute-start | bytes 2654216 | tf_op jit(solution)/shard_map/ppermute | solution.py:35
  368.7 29.9 %collective-permute-start.65 = (bf16[2,864,128]{2,1,0:T(8,128)(2,1)S(1)}, bf16[2,864,128]{2,1,0:T(8,128)(2,1)S(1)}, u32[]{:S(2)}, u32[]{:S(2)}) collective-permute-start(bf16[2,864,128]{2,1,0:T(8,128)(2,1)S(1)} %fusion.20), channel_id=1, source_target_pairs={{0,4},{2,6},{4,0},{6,2},{8,12},{10,14},{12,8},{14,10},{16,20},{18,... | collective-permute-start | bytes 1327112 | tf_op jit(solution)/shard_map/ppermute | solution.py:35
  370.1 38.8 %collective-permute-start.67 = (bf16[2,864,128]{2,1,0:T(8,128)(2,1)}, bf16[2,864,128]{2,1,0:T(8,128)(2,1)S(1)}, u32[]{:S(2)}, u32[]{:S(2)}) collective-permute-start(bf16[2,864,128]{2,1,0:T(8,128)(2,1)} %fusion.21), channel_id=1, source_target_pairs={{0,2},{2,0},{4,6},{6,4},{8,10},{10,8},{12,14},{14,12},{16,18},{18,... | collective-permute-start | bytes 1327112 | tf_op jit(solution)/shard_map/ppermute | solution.py:35
  387.6 22.7 %collective-permute-start.57 = (bf16[2,864,128]{2,1,0:T(8,128)(2,1)}, bf16[2,864,128]{2,1,0:T(8,128)(2,1)}, u32[]{:S(2)}, u32[]{:S(2)}) collective-permute-start(bf16[2,864,128]{2,1,0:T(8,128)(2,1)} %fusion.18), channel_id=1, source_target_pairs={{0,4},{2,6},{4,0},{6,2},{8,12},{10,14},{12,8},{14,10},{16,20},{18,... | collective-permute-start | bytes 1327112 | tf_op jit(solution)/shard_map/ppermute | solution.py:35
  389.1 24.4 %collective-permute-start.59 = (bf16[2,864,128]{2,1,0:T(8,128)(2,1)}, bf16[2,864,128]{2,1,0:T(8,128)(2,1)}, u32[]{:S(2)}, u32[]{:S(2)}) collective-permute-start(bf16[2,864,128]{2,1,0:T(8,128)(2,1)} %fusion.19), channel_id=1, source_target_pairs={{0,2},{2,0},{4,6},{6,4},{8,10},{10,8},{12,14},{14,12},{16,18},{18,... | collective-permute-start | bytes 1327112 | tf_op jit(solution)/shard_map/ppermute | solution.py:35
  417.6 43.7 %collective-permute-start.68 = (bf16[2,864,128]{2,1,0:T(8,128)(2,1)S(1)}, bf16[2,864,128]{2,1,0:T(8,128)(2,1)S(1)}, u32[]{:S(2)}, u32[]{:S(2)}) collective-permute-start(bf16[2,864,128]{2,1,0:T(8,128)(2,1)S(1)} %dynamic-slice_bitcast_fusion.4), channel_id=1, source_target_pairs={{0,8},{2,10},{4,12},{6,14},{8,0},{10,2},{12,4},{14,6},{16,24},{18,... | collective-permute-start | bytes 1327112 | tf_op jit(solution)/shard_map/ppermute | solution.py:35
  420.6 40.0 %collective-permute-start.35 = (bf16[2,17,160,128]{3,2,1,0:T(8,128)(2,1)S(1)}, bf16[2,17,160,128]{3,2,1,0:T(8,128)(2,1)S(1)}, u32[]{:S(2)}, u32[]{:S(2)}) collective-permute-start(bf16[2,17,160,128]{3,2,1,0:T(8,128)(2,1)S(1)} %dynamic-slice_bitcast_fusion), channel_id=1, source_target_pairs={{0,8},{2,10},{4,12},{6,14},{8,0},{10,2},{12,4},{14,6},{16,24},{18,... | collective-permute-start | bytes 4177928 | tf_op jit(solution)/shard_map/ppermute | solution.py:35
  422.7 67.0 %collective-permute-start.60 = (bf16[2,864,128]{2,1,0:T(8,128)(2,1)S(1)}, bf16[2,864,128]{2,1,0:T(8,128)(2,1)S(1)}, u32[]{:S(2)}, u32[]{:S(2)}) collective-permute-start(bf16[2,864,128]{2,1,0:T(8,128)(2,1)S(1)} %dynamic-slice_bitcast_fusion.5), channel_id=1, source_target_pairs={{0,8},{2,10},{4,12},{6,14},{8,0},{10,2},{12,4},{14,6},{16,24},{18,... | collective-permute-start | bytes 1327112 | tf_op jit(solution)/shard_map/ppermute | solution.py:35
  426.5 78.4 %collective-permute-start.52 = (bf16[2,864,128]{2,1,0:T(8,128)(2,1)S(1)}, bf16[2,864,128]{2,1,0:T(8,128)(2,1)S(1)}, u32[]{:S(2)}, u32[]{:S(2)}) collective-permute-start(bf16[2,864,128]{2,1,0:T(8,128)(2,1)S(1)} %dynamic-slice_bitcast_fusion.6), channel_id=1, source_target_pairs={{0,8},{2,10},{4,12},{6,14},{8,0},{10,2},{12,4},{14,6},{16,24},{18,... | collective-permute-start | bytes 1327112 | tf_op jit(solution)/shard_map/ppermute | solution.py:35
  427.1 79.8 %collective-permute-start.20 = (bf16[2,864,128]{2,1,0:T(8,128)(2,1)S(1)}, bf16[2,864,128]{2,1,0:T(8,128)(2,1)S(1)}, u32[]{:S(2)}, u32[]{:S(2)}) collective-permute-start(bf16[2,864,128]{2,1,0:T(8,128)(2,1)S(1)} %dynamic-slice_bitcast_fusion.7), channel_id=1, source_target_pairs={{0,8},{2,10},{4,12},{6,14},{8,0},{10,2},{12,4},{14,6},{16,24},{18,... | collective-permute-start | bytes 1327112 | tf_op jit(solution)/shard_map/ppermute | solution.py:35
  461.0 40.5 %collective-permute-start.36 = (bf16[1,17,160,128]{3,2,1,0:T(8,128)(2,1)S(1)}, bf16[1,17,160,128]{3,2,1,0:T(8,128)(2,1)S(1)}, u32[]{:S(2)}, u32[]{:S(2)}) collective-permute-start(bf16[1,17,160,128]{3,2,1,0:T(8,128)(2,1)S(1)} %constant_dynamic-slice_fusion.9), channel_id=1, source_target_pairs={{0,16},{2,18},{4,20},{6,22},{8,24},{10,26},{12,28},{14,30},{16,0},... | collective-permute-start | bytes 2088968 | tf_op jit(solution)/shard_map/ppermute | solution.py:35
  461.5 74.5 %collective-permute-start.69 = (bf16[1,864,128]{2,1,0:T(8,128)(2,1)S(1)}, bf16[1,864,128]{2,1,0:T(8,128)(2,1)S(1)}, u32[]{:S(2)}, u32[]{:S(2)}) collective-permute-start(bf16[1,864,128]{2,1,0:T(8,128)(2,1)S(1)} %constant_dynamic-slice_fusion), channel_id=1, source_target_pairs={{0,16},{2,18},{4,20},{6,22},{8,24},{10,26},{12,28},{14,30},{16,0},... | collective-permute-start | bytes 663560 | tf_op jit(solution)/shard_map/ppermute | solution.py:35
  503.2 28.9 %collective-permute-start.38 = (bf16[17,160,128]{2,1,0:T(8,128)(2,1)S(1)}, bf16[17,160,128]{2,1,0:T(8,128)(2,1)S(1)}, u32[]{:S(2)}, u32[]{:S(2)}) collective-permute-start(bf16[17,160,128]{2,1,0:T(8,128)(2,1)S(1)} %get-tuple-element.53), channel_id=1, source_target_pairs={{0,4},{2,6},{4,0},{6,2},{8,12},{10,14},{12,8},{14,10},{16,20},{18,... | collective-permute-start | bytes 2088968 | tf_op jit(solution)/shard_map/ppermute | solution.py:35
  504.9 30.5 %collective-permute-start.37 = (bf16[17,160,128]{2,1,0:T(8,128)(2,1)S(1)}, bf16[17,160,128]{2,1,0:T(8,128)(2,1)S(1)}, u32[]{:S(2)}, u32[]{:S(2)}) collective-permute-start(bf16[17,160,128]{2,1,0:T(8,128)(2,1)S(1)} %get-tuple-element.53), channel_id=1, source_target_pairs={{0,2},{2,0},{4,6},{6,4},{8,10},{10,8},{12,14},{14,12},{16,18},{18,... | collective-permute-start | bytes 2088968 | tf_op jit(solution)/shard_map/ppermute | solution.py:35
  506.8 29.3 %collective-permute-start.61 = (bf16[1,864,128]{2,1,0:T(8,128)(2,1)S(1)}, bf16[1,864,128]{2,1,0:T(8,128)(2,1)S(1)}, u32[]{:S(2)}, u32[]{:S(2)}) collective-permute-start(bf16[1,864,128]{2,1,0:T(8,128)(2,1)S(1)} %constant_dynamic-slice_fusion.1), channel_id=1, source_target_pairs={{0,16},{2,18},{4,20},{6,22},{8,24},{10,26},{12,28},{14,30},{16,0},... | collective-permute-start | bytes 663560 | tf_op jit(solution)/shard_map/ppermute | solution.py:35
  532.1 28.6 %collective-permute-start.21 = (bf16[1,864,128]{2,1,0:T(8,128)(2,1)S(1)}, bf16[1,864,128]{2,1,0:T(8,128)(2,1)S(1)}, u32[]{:S(2)}, u32[]{:S(2)}) collective-permute-start(bf16[1,864,128]{2,1,0:T(8,128)(2,1)S(1)} %constant_dynamic-slice_fusion.17), channel_id=1, source_target_pairs={{0,16},{2,18},{4,20},{6,22},{8,24},{10,26},{12,28},{14,30},{16,0},... | collective-permute-start | bytes 663560 | tf_op jit(solution)/shard_map/ppermute | solution.py:35
  535.9 85.8 %collective-permute-start.40 = (bf16[4,17,160,128]{3,2,0,1:T(8,128)(2,1)S(1)}, bf16[4,17,160,128]{3,2,0,1:T(8,128)(2,1)}, u32[]{:S(2)}, u32[]{:S(2)}) collective-permute-start(bf16[4,17,160,128]{3,2,0,1:T(8,128)(2,1)S(1)} %get-tuple-element.42), channel_id=1, source_target_pairs={{0,1},{1,0},{2,3},{3,2},{4,5},{5,4},{6,7},{7,6},{8,9},{9,8},{10,11... | collective-permute-start | bytes 8355848 | tf_op jit(solution)/shard_map/ppermute | solution.py:35
  536.1 34.0 %collective-permute-start.70 = (bf16[1,864,128]{2,1,0:T(8,128)(2,1)S(1)}, bf16[1,864,128]{2,1,0:T(8,128)(2,1)S(1)}, u32[]{:S(2)}, u32[]{:S(2)}) collective-permute-start(bf16[1,864,128]{2,1,0:T(8,128)(2,1)S(1)} %add_convert_fusion.12), channel_id=1, source_target_pairs={{0,16},{2,18},{4,20},{6,22},{8,24},{10,26},{12,28},{14,30},{16,0},... | collective-permute-start | bytes 663560 | tf_op jit(solution)/shard_map/ppermute | solution.py:35
  536.2 38.7 %collective-permute-start.62 = (bf16[1,864,128]{2,1,0:T(8,128)(2,1)S(1)}, bf16[1,864,128]{2,1,0:T(8,128)(2,1)S(1)}, u32[]{:S(2)}, u32[]{:S(2)}) collective-permute-start(bf16[1,864,128]{2,1,0:T(8,128)(2,1)S(1)} %add_convert_fusion.13), channel_id=1, source_target_pairs={{0,16},{2,18},{4,20},{6,22},{8,24},{10,26},{12,28},{14,30},{16,0},... | collective-permute-start | bytes 663560 | tf_op jit(solution)/shard_map/ppermute | solution.py:35
  539.3 40.4 %collective-permute-start.54 = (bf16[1,864,128]{2,1,0:T(8,128)(2,1)S(1)}, bf16[1,864,128]{2,1,0:T(8,128)(2,1)S(1)}, u32[]{:S(2)}, u32[]{:S(2)}) collective-permute-start(bf16[1,864,128]{2,1,0:T(8,128)(2,1)S(1)} %add_convert_fusion.14), channel_id=1, source_target_pairs={{0,16},{2,18},{4,20},{6,22},{8,24},{10,26},{12,28},{14,30},{16,0},... | collective-permute-start | bytes 663560 | tf_op jit(solution)/shard_map/ppermute | solution.py:35
  560.7 23.1 %collective-permute-start.22 = (bf16[1,864,128]{2,1,0:T(8,128)(2,1)S(1)}, bf16[1,864,128]{2,1,0:T(8,128)(2,1)S(1)}, u32[]{:S(2)}, u32[]{:S(2)}) collective-permute-start(bf16[1,864,128]{2,1,0:T(8,128)(2,1)S(1)} %add_convert_fusion.16), channel_id=1, source_target_pairs={{0,16},{2,18},{4,20},{6,22},{8,24},{10,26},{12,28},{14,30},{16,0},... | collective-permute-start | bytes 663560 | tf_op jit(solution)/shard_map/ppermute | solution.py:35
  570.2 23.1 %collective-permute-start.71 = (bf16[2,864,128]{2,1,0:T(8,128)(2,1)S(1)}, bf16[2,864,128]{2,1,0:T(8,128)(2,1)S(1)}, u32[]{:S(2)}, u32[]{:S(2)}) collective-permute-start(bf16[2,864,128]{2,1,0:T(8,128)(2,1)S(1)} %pad_maximum_fusion.19), channel_id=1, source_target_pairs={{0,8},{2,10},{4,12},{6,14},{8,0},{10,2},{12,4},{14,6},{16,24},{18,... | collective-permute-start | bytes 1327112 | tf_op jit(solution)/shard_map/ppermute | solution.py:35
  575.0 27.8 %collective-permute-start.63 = (bf16[2,864,128]{2,1,0:T(8,128)(2,1)S(1)}, bf16[2,864,128]{2,1,0:T(8,128)(2,1)S(1)}, u32[]{:S(2)}, u32[]{:S(2)}) collective-permute-start(bf16[2,864,128]{2,1,0:T(8,128)(2,1)S(1)} %pad_maximum_fusion.18), channel_id=1, source_target_pairs={{0,8},{2,10},{4,12},{6,14},{8,0},{10,2},{12,4},{14,6},{16,24},{18,... | collective-permute-start | bytes 1327112 | tf_op jit(solution)/shard_map/ppermute | solution.py:35
  579.7 32.5 %collective-permute-start.55 = (bf16[2,864,128]{2,1,0:T(8,128)(2,1)S(1)}, bf16[2,864,128]{2,1,0:T(8,128)(2,1)S(1)}, u32[]{:S(2)}, u32[]{:S(2)}) collective-permute-start(bf16[2,864,128]{2,1,0:T(8,128)(2,1)S(1)} %pad_maximum_fusion.17), channel_id=1, source_target_pairs={{0,8},{2,10},{4,12},{6,14},{8,0},{10,2},{12,4},{14,6},{16,24},{18,... | collective-permute-start | bytes 1327112 | tf_op jit(solution)/shard_map/ppermute | solution.py:35
  583.9 37.8 %collective-permute-start.23 = (bf16[2,864,128]{2,1,0:T(8,128)(2,1)S(1)}, bf16[2,864,128]{2,1,0:T(8,128)(2,1)S(1)}, u32[]{:S(2)}, u32[]{:S(2)}) collective-permute-start(bf16[2,864,128]{2,1,0:T(8,128)(2,1)S(1)} %pad_maximum_fusion.16), channel_id=1, source_target_pairs={{0,8},{2,10},{4,12},{6,14},{8,0},{10,2},{12,4},{14,6},{16,24},{18,... | collective-permute-start | bytes 1327112 | tf_op jit(solution)/shard_map/ppermute | solution.py:35
  (64 other events, 1280.1 us)

commit v2 on v1

--- a/solution.py
+++ b/solution.py
@@ -44,6 +44,10 @@
     return x
 
 
+def after(x, *done):
+    return lax.optimization_barrier((x,) + done)[0]
+
+
 def add(*terms):
     total = terms[0].astype(F32)
     for term in terms[1:]:
@@ -61,7 +65,60 @@
     return jnp.concatenate(shares, axis=0) if len(shares) > 1 else shares[0]
 
 
-def rotate_in_kernel(n, blocks, position, *refs):
+def split_kernel(pieces, where, *refs):
+    sources, outs = refs[: -len(pieces)], refs[-len(pieces) :]
+    xy = where[0] % INNER
+    for v in range(INNER):
+
+        @pl.when(xy == v)
+        def _(v=v):
+            for r, out in enumerate(outs):
+                at = 0
+                for start, stop in pieces[r ^ v]:
+                    for s, source in enumerate(sources):
+                        out[s, :, at : at + stop - start] = source[:, start:stop]
+                    at += stop - start
+
+
+def split(where, sources, pieces):
+    rows = sources[0].shape[0]
+    width = sum(stop - start for start, stop in pieces[0])
+    shape = jax.ShapeDtypeStruct((len(sources), rows, width), sources[0].dtype)
+    return pl.pallas_call(
+        functools.partial(split_kernel, pieces),
+        out_shape=[shape] * len(pieces),
+        in_specs=[SMEM] + [VMEM] * len(sources),
+        out_specs=[VMEM] * len(pieces),
+        compiler_params=pltpu.CompilerParams(vmem_limit_bytes=40 << 20),
+        cost_estimate=pl.CostEstimate(
+            flops=0, bytes_accessed=4 * len(sources) * sources[0].size, transcendentals=0
+        ),
+    )(where, *sources)
+
+
+def invert_kernel(*refs):
+    sources, out = refs[:-1], refs[-1]
+    rows = sources[0].shape[1]
+    for r, source in enumerate(sources):
+        damped = source[0].astype(F32) + DAMPING
+        out[:, r * rows : (r + 1) * rows] = (1.0 / damped).T
+
+
+def invert(sources):
+    _, rows, cols = sources[0].shape
+    return pl.pallas_call(
+        invert_kernel,
+        out_shape=jax.ShapeDtypeStruct((cols, len(sources) * rows), F32),
+        in_specs=[VMEM] * len(sources),
+        out_specs=VMEM,
+        compiler_params=pltpu.CompilerParams(vmem_limit_bytes=40 << 20),
+        cost_estimate=pl.CostEstimate(
+            flops=8 * rows * cols, bytes_accessed=24 * rows * cols, transcendentals=0
+        ),
+    )(*sources)
+
+
+def rotate_in_kernel(n, blocks, outer, *refs):
     where, query, basis, parts, out = refs[0], refs[1], refs[2], refs[3:-1], refs[-1]
     me, e = where[0], where[1]
     width = basis.shape[0] // blocks
@@ -76,7 +133,10 @@
 
     @pl.loop(0, n // 4)
     def _(step):
-        rows = [group_rows(parts, e, position((step * 4 + p) ^ me)) for p in range(4)]
+        rows = []
+        for p in range(4):
+            rel = (step * 4 + p) ^ me
+            rows.append(group_rows(parts, e, (rel % INNER) * outer + rel // INNER))
         product = lax.dot_general(
             basis[...], jnp.concatenate(rows, axis=0), NT, preferred_element_type=F32
         )
@@ -84,10 +144,10 @@
             store(step * 4 + p, product, p)
 
 
-def rotate_in(where, query, basis, parts, n, blocks, position):
+def rotate_in(where, query, basis, parts, n, blocks, outer):
     width = basis.shape[0] // blocks
     return pl.pallas_call(
-        functools.partial(rotate_in_kernel, n, blocks, position),
+        functools.partial(rotate_in_kernel, n, blocks, outer),
         out_shape=jax.ShapeDtypeStruct((blocks, n + 1, width, TOK_DEV), BF16),
         in_specs=[SMEM] + [VMEM] * (2 + len(parts)),
         out_specs=VMEM,
@@ -101,13 +161,19 @@
 
 
 def rotate_out_kernel(chunk, outer, where, basis, *refs):
-    parts, (sx, kx, sy, ky) = refs[:-4], refs[-4:]
+    parts, (sx, kx, sy, ky), rows = refs[:-5], refs[-5:-1], refs[-1]
     me, e = where[0], where[1]
     half = outer // 2
-    rows = [group_rows(parts, e, (chunk * outer + p) ^ me) for p in range(outer)]
-    product = lax.dot_general(
-        basis[0], jnp.concatenate(rows, axis=0), NT, preferred_element_type=F32
-    )
+
+    @pl.when(pl.program_id(0) == 0)
+    def _():
+        for p in range(outer):
+            rel = (chunk * outer + p) ^ me
+            rows[p * TOK_DEV : (p + 1) * TOK_DEV] = group_rows(
+                parts, e, (rel % INNER) * outer + rel // INNER
+            )
+
+    product = lax.dot_general(basis[0], rows[...], NT, preferred_element_type=F32)
     low = [product[:, p * TOK_DEV : (p + 1) * TOK_DEV].astype(BF16) for p in range(half)]
     high = [
         product[:, p * TOK_DEV : (p + 1) * TOK_DEV].astype(BF16) for p in range(half, outer)
@@ -141,6 +207,7 @@
             in_specs=[pl.BlockSpec((1, cols, depth), lambda r, w: (r ^ (w[0] % INNER), 0, 0))]
             + [pl.BlockSpec(part.shape, lambda r, w: (0, 0, 0)) for part in parts],
             out_specs=[kept] * 4,
+            scratch_shapes=[pltpu.VMEM((outer * TOK_DEV, depth), BF16)],
         ),
         compiler_params=pltpu.CompilerParams(vmem_limit_bytes=40 << 20),
         cost_estimate=pl.CostEstimate(
@@ -151,43 +218,59 @@
     )(where, basis, *parts)
 
 
-def score_kernel(chunk, outer, masks, where, b_ref, a_ref, inverse, query_b, seq, out):
-    z = where[0] // INNER
-    count, rows = a_ref.shape[0] - 1, a_ref.shape[1]
+def score_kernel(chunk, outer, masks, shares, where, b_ref, inverse, query_b, seq, *refs):
+    a_refs, out, a_all = refs[:shares], refs[shares], refs[shares + 1]
+    z, e = where[0] // INNER, where[1]
+    count, rows = a_refs[0].shape[1] - 1, a_all.shape[1]
+    width = a_refs[0].shape[2]
     tile = 256 if rows % 256 == 0 else 128
+
+    def gather(group, slot):
+        for r in range(INNER):
+            for h in range(shares):
+                a = a_refs[0][r, group]
+                for m in range(1, shares):
+                    a = jnp.where((e ^ m) == h, a_refs[m][r, group], a)
+                start = (r * shares + h) * width
+                a_all[slot, start : start + width] = a
+
+    gather(count, len(masks))
     for p, mask in enumerate(masks):
         place = z ^ mask
         group = chunk * outer + place
+        gather(group, p)
         for member in range(SEQ_DEV):
             b = jnp.where(seq[group] == member, b_ref[p].astype(F32), 0.0).astype(BF16)
             total = jnp.zeros((b.shape[0], TOK_DEV), F32)
             for start in range(0, rows, tile):
                 grad = lax.dot_general(
-                    b, a_ref[group, start : start + tile], NT, preferred_element_type=F32
+                    b, a_all[p, start : start + tile], NT, preferred_element_type=F32
                 )
                 scaled = (grad * inverse[:, start : start + tile]).astype(BF16)
                 total = total + jnp.dot(
-                    scaled, a_ref[count, start : start + tile], preferred_element_type=F32
+                    scaled,
+                    a_all[len(masks), start : start + tile],
+                    preferred_element_type=F32,
                 )
-            out[place, member : member + 1] = jnp.sum(
-                total * query_b[...], axis=0, keepdims=True
-            )
-
-
-def score(where, b, a, inverse, query_b, seq, chunk, outer, masks):
+            out[p, member : member + 1] = jnp.sum(total * query_b[...], axis=0, keepdims=True)
+
+
+def score(where, b, a_parts, inverse, query_b, seq, chunk, outer, masks):
     cols, rows = inverse.shape
+    count = len(masks)
     return pl.pallas_call(
-        functools.partial(score_kernel, chunk, outer, masks),
-        out_shape=jax.ShapeDtypeStruct((outer, SEQ_DEV, TOK_DEV), F32),
-        in_specs=[SMEM] + [VMEM] * 5,
+        functools.partial(score_kernel, chunk, outer, masks, len(a_parts)),
+        out_shape=jax.ShapeDtypeStruct((count, SEQ_DEV, TOK_DEV), F32),
+        in_specs=[SMEM] + [VMEM] * (4 + len(a_parts)),
         out_specs=VMEM,
+        scratch_shapes=[pltpu.VMEM((count + 1, rows, TOK_DEV), BF16)],
         compiler_params=pltpu.CompilerParams(vmem_limit_bytes=48 << 20),
         cost_estimate=pl.CostEstimate(
-            flops=8 * outer * SEQ_DEV * TOK_DEV * cols * rows,
-            bytes_accessed=2 * (b.size + a.size + 2 * inverse.size),
+            flops=16 * count * SEQ_DEV * TOK_DEV * cols * rows,
+            bytes_accessed=2 * (b.size + 2 * a_parts[0].size + 2 * inverse.size),
             transcendentals=0,
         ),
-    )(where, b, a, inverse, query_b, seq)
+    )(where, b, inverse, query_b, seq, *a_parts)
 
 
 def body(
@@ -214,12 +297,17 @@
     rows_in = rows_own * INNER
     per_core = input_basis.shape[1] // rows_in
 
-    own = lax.dynamic_slice_in_dim(train_out, e * share, share, 0)
-    own = own.reshape(share, n, depth_out).transpose(1, 0, 2)
-    out_rel = jnp.stack(
-        [pick(own, me)] + [swap(pick(own, me ^ m), "seq", m) for m in range(1, n)]
-    )
-    out_parts = [out_rel] + [swap(out_rel, "eig", m) for m in range(1, size)]
+    def to_planes(x, width):
+        pieces = [
+            lax.dynamic_slice(x, (e * share, (z ^ m) * width), (share, width))
+            for m in range(outer)
+        ]
+        return pieces[:1] + [
+            swap(pieces[m], "seq", m * INNER) for m in range(1, outer)
+        ]
+
+    def in_plane(pieces):
+        return [pieces[0]] + [swap(pieces[r], "seq", r) for r in range(1, INNER)]
 
     small = jnp.concatenate(
         [
@@ -229,40 +317,59 @@
             (query_order % QUERIES).astype(BF16)[:, None],
         ],
         axis=1,
+    )[None]
+
+    def grow(x, b, axis):
+        other = swap(x, "seq", 1 << b)
+        upper = (me >> b) & 1 == 1
+        return jnp.concatenate(
+            [jnp.where(upper, other, x), jnp.where(upper, x, other)], axis=axis
+        )
+
+    for b in range(INNER.bit_length() - 1, n.bit_length() - 1):
+        small = grow(small, b, 0)
+
+    in_pieces = to_planes(train_in, rows_in)
+    out_pieces = to_planes(after(train_out, *in_pieces[1:]), INNER * depth_out)
+
+    basis_pieces = in_plane(
+        split(
+            where,
+            [input_basis],
+            [
+                [
+                    ((k * INNER + a) * rows_own, (k * INNER + a + 1) * rows_own)
+                    for k in range(per_core)
+                ]
+                for a in range(INNER)
+            ],
+        )
     )
-    small = lax.all_gather(small, "seq", axis=0, tiled=True)
+
+    small = small[:, None]
+    for b in bits(INNER):
+        small = grow(small, b, 1)
+    small = small.reshape(n * query_rows, -1)
     din, dout = query_in.shape[1], query_out.shape[1]
     seq = small[:, din + dout : -1].reshape(n, 1, TOK_DEV).astype(F32)
     labels = small[:, -1].astype(F32)
     hot = (labels[:, None] == jnp.arange(QUERIES, dtype=F32)[None, :]).astype(F32)
     queries = small.shape[0]
 
-    blocks = input_basis.reshape(rows_own, per_core, INNER, rows_own).transpose(2, 0, 1, 3)
-    blocks = blocks.reshape(INNER, rows_own, per_core * rows_own)
-    basis_in = jnp.stack(
-        [pick(blocks, xy)] + [swap(pick(blocks, xy ^ r), "seq", r) for r in range(1, INNER)]
-    )
-    basis_in = unxor(basis_in, xy).reshape(rows_in, -1).T
-
-    own = lax.dynamic_slice_in_dim(train_in, e * share, share, 0)
-    own = own.reshape(share, outer, rows_in).transpose(1, 0, 2)
-    in_rel = jnp.stack(
-        [pick(own, z)]
-        + [swap(pick(own, z ^ m), "seq", m * INNER) for m in range(1, outer)]
-    )
-    in_rel = jnp.concatenate([in_rel] + [swap(in_rel, "seq", r) for r in range(1, INNER)])
+    in_rel = after(jnp.stack(in_pieces), *basis_pieces[1:])
+    in_rel = jnp.concatenate(in_plane([in_rel] * INNER))
     in_parts = [in_rel] + [swap(in_rel, "eig", m) for m in range(1, size)]
+
+    quarter = [[(a * cols_own, (a + 1) * cols_own)] for a in range(INNER)]
+    inverse = invert(in_plane(split(where, [after(corrected, in_rel)], quarter)))
+
+    out_rel = jnp.concatenate(in_plane(split(where, out_pieces, [[(a * depth_out, (a + 1) * depth_out)] for a in range(INNER)])))
+    out_parts = [out_rel] + [swap(out_rel, "eig", m) for m in range(1, size)]
+
+    basis_in = unxor(jnp.concatenate(basis_pieces), xy).reshape(rows_in, -1).T
     query_rows_in = lax.dynamic_slice_in_dim(small, z * rows_in, rows_in, 1)
     query_rows_in = jnp.pad(query_rows_in, ((0, TOK_DEV - queries), (0, 0)))
-    rotated = rotate_in(
-        where,
-        query_rows_in,
-        basis_in,
-        in_parts,
-        n,
-        per_core,
-        lambda rel: (rel % INNER) * outer + rel // INNER,
-    )
+    rotated = rotate_in(where, query_rows_in, basis_in, in_parts, n, per_core, outer)
     rotated = rotated.reshape(per_core, n + 1, size, rows_own // size, TOK_DEV)
     rotated = jnp.stack(
         [pick(rotated, e, 2)]
@@ -276,15 +383,6 @@
             pick(pairs, bit, 1), swap(pick(pairs, 1 - bit, 1), "seq", INNER << b)
         )
     rotated = rotated[0]
-    rotated = jnp.stack([rotated] + [swap(rotated, "seq", r) for r in range(1, INNER)])
-    rotated = jnp.stack([rotated] + [swap(rotated, "eig", m) for m in range(1, size)])
-    full_a = unxor(rotated, e).transpose(2, 1, 0, 3, 4).reshape(n + 1, rows_in, TOK_DEV)
-
-    blocks = corrected.reshape(rows_own, INNER, cols_own).transpose(1, 0, 2)
-    piece = jnp.concatenate(
-        [pick(blocks, xy)] + [swap(pick(blocks, xy ^ r), "seq", r) for r in range(1, INNER)]
-    )
-    inverse = 1.0 / (piece.T.astype(F32) + DAMPING)
 
     query_b = lax.dynamic_slice_in_dim(small, din + me * depth_out, depth_out, 1)
     query_b = jnp.dot(query_b, output_basis, preferred_element_type=F32).astype(BF16)
@@ -297,10 +395,22 @@
     found = []
     for chunk in range(INNER):
         sx, kx, sy, ky = rotate_out(where, basis_out, out_parts, chunk, outer)
+        if chunk > 0:
+            sx, sy = after((sx, sy), rx, ry)
+        if chunk == 2:
+            sx, sy = after((sx, sy), a_parts[0])
         rx, ry = swap(sx, "seq", 1), swap(sy, "seq", 2)
+        if chunk == 0:
+            a_parts = jnp.stack(in_plane([after(rotated, rx, ry)] * INNER))
+            a_parts = [a_parts] + [swap(a_parts, "eig", m) for m in range(1, size)]
+            if a_parts[0].shape[2] % 16:
+                whole = unxor(jnp.stack(a_parts), e).transpose(1, 2, 0, 3, 4)
+                a_parts = [whole.reshape(INNER, n + 1, rows_own, TOK_DEV)]
         low = add(kx[0], rx[0], swap(add(kx[1], rx[1]), "seq", 2))
         high = add(ky[0], ry[0], swap(add(ky[1], ry[1]), "seq", 1))
         held = jnp.concatenate([low, high])
+        if chunk == 0:
+            held = after(held, rotated)
         for b in bits(outer):
             bit = (z >> b) & 1
             pairs = held.reshape((-1, 2) + held.shape[1:])
@@ -308,13 +418,29 @@
                 pick(pairs, bit, 1), swap(pick(pairs, 1 - bit, 1), "seq", INNER << b)
             )
         masks = [0]
+        scored = []
         for b in reversed(bits(outer)):
-            held = jnp.concatenate([held, swap(held, "seq", INNER << b)])
-            masks = masks + [m | (1 << b) for m in masks]
-        found.append(
-            score(where, held, full_a, inverse, query_b, seq, chunk, outer, masks)
-        )
-    per_token = jnp.concatenate(found)[:, :, :queries]
+            other = swap(held, "seq", INNER << b)
+            new = [m | (1 << b) for m in masks]
+            if b == 0:
+                scored.append((held, masks))
+                scored.append((other, new))
+            else:
+                held = jnp.concatenate([held, other])
+                masks = masks + new
+        parts = []
+        order = []
+        for b_part, b_masks in scored:
+            parts.append(
+                score(
+                    where, b_part, a_parts, inverse, query_b, seq, chunk, outer, b_masks
+                )
+            )
+            order += b_masks
+        parts = jnp.concatenate(parts)[:, :, :queries]
+        parts = jnp.stack([parts[order.index(m)] for m in range(outer)])
+        found.append(unxor(parts, z))
+    per_token = jnp.concatenate(found)
     scores = jnp.sum(per_token[:, :, :, None] * hot[None, None], axis=2)
     scores = lax.all_to_all(scores, "seq", split_axis=0, concat_axis=0, tiled=True)
     scores = jnp.sum(scores, axis=0)

time: 703 us -> 534 us (0.76)
  local copies, waits for them, and re-layouts: 137 us -> 69.2 us
  waiting for transfers between devices: 267 us -> 207 us
  blocking collectives: 62 us -> 14.6 us
  Pallas kernels: 90.2 us -> 111 us
  other arithmetic: 48.4 us -> 32.2 us
    ppermute x73 -> x68, waiting for transfers between devices: 267 us -> 207 us  [swap(): return lax.ppermute(x, axis, [(i, i ^ mask) for i in range(size)])]
    all_gather x1 -> x0, blocking collectives: 51.4 us -> none  [body(): small = lax.all_gather(small, 'seq', axis=0, tiled=True)]
    unnamed x125 -> x67, local copies, waits for them, and re-layouts: 58 us -> 30.4 us
    pallas_call x5 -> x13, Pallas kernels: 57 us -> 81.7 us  [the longest x8 68.4 us: score(): pl.pallas_call(functools.partial(score_kernel, chunk, outer, masks, len(a...]
    reshape x6 -> x1, local copies, waits for them, and re-layouts: 18.9 us -> 1.32 us  [body(): small = small.reshape(n * query_rows, -1)]
    another operation x4 -> x1, local copies, waits for them, and re-layouts: 14.7 us -> 2 us  [body(): in_rel = after(jnp.stack(in_pieces), *basis_pieces[1:])]
    convert_element_type x30 -> x29, other arithmetic: 24.6 us -> 14.5 us  [add(): return total.astype(BF16)]
    ppermute x73 -> x68, starting transfers between devices: 87.3 us -> 83.7 us  [swap(): return lax.ppermute(x, axis, [(i, i ^ mask) for i in range(size)])]
  transfers between devices with their start and end apart: 73 -> 68, of which waited for: 36 -> 29; matrix products, arithmetic and copies ran while one was open for 23% -> 18% of each run, Pallas kernels for 6% -> 20%
where the time goes in v2:
time: 534 us; the launch traced here: 524 us
  waiting for transfers between devices  207 us (39%)
  Pallas kernels  111 us (21%)
  starting transfers between devices  83.7 us (16%)
  local copies, waits for them, and re-layouts  69.2 us (13%)
  other arithmetic  32.2 us (6%)
  blocking collectives  14.6 us (3%)
    ppermute x68, waiting for transfers between devices, swap(): return lax.ppermute(x, axis, [(i, i ^ mask) for i in range(size)])  207 us
    ppermute x68, starting transfers between devices, swap(): return lax.ppermute(x, axis, [(i, i ^ mask) for i in range(size)])  83.7 us
    pallas_call x8, Pallas kernels, score(): pl.pallas_call(functools.partial(score_kernel, chunk, outer, masks, len(a...  68.4 us
    unnamed x67, local copies, waits for them, and re-layouts  30.4 us
    pallas_call x4, Pallas kernels, rotate_out(): pl.pallas_call(functools.partial(rotate_out_kernel, chunk, outer), out_sh...  29 us
    all_to_all x1, blocking collectives, body(): lax.all_to_all(scores, 'seq', split_axis=0, concat_axis=0, tiled=True)  14.6 us
    convert_element_type x29, other arithmetic, add(): return total.astype(BF16)  14.5 us
  transfers between devices with their start and end apart: 68, of which 29 were waited for; matrix products, arithmetic and copies ran while one was open for 18% of the time, Pallas kernels for 20%

profile of v2, /device:TPU:0, one launch (start us, length us, event | category | flops | bytes accessed | tf_op | source)
XLA Modules:
  0.0 524.0 jit_solution(5573036872436569731)
XLA Ops:
  2.2 3.1 collective-permute-start.14
  7.4 3.0 collective-permute-start.1
  15.7 9.2 %copy.138 = bf16[864,3456]{0,1:T(8,128)(2,1)} copy(bf16[864,3456]{1,0:T(8,128)(2,1)} %param.14) | data formatting | bytes 11943936 | tf_op args[5]
  27.1 4.0 collective-permute-done.15
  35.1 2.5 fusion.29
  39.7 5.4 %collective-permute-done.16 = bf16[4,1,1,19073]{3,0,2,1:T(4,128)(2,1)S(1)} collective-permute-done((bf16[4,1,1,19073]{3,0,2,1:T(4,128)(2,1)S(1)}, bf16[4,1,1,19073]{3,0,2,1:T(4,128)(2,1)S(1)}, u32[]{:S(2)}, u32[]{:S(2)}) %collective-permute-start.16) | collective-permute-done | bytes 152616 | tf_op jit(solution)/shard_map/ppermute | solution.py:35
  47.8 3.8 collective-permute-done.19
  52.7 2.4 collective-permute-start.23
  58.7 3.7 copy.147
  63.7 3.7 copy.145
  77.5 3.9 convolution_convert_fusion
  101.3 10.7 %collective-permute-done.4.refs_2_ = bf16[64,3456]{1,0:T(8,128)(2,1)S(1)} collective-permute-done((bf16[64,3456]{1,0:T(8,128)(2,1)}, bf16[64,3456]{1,0:T(8,128)(2,1)S(1)}, u32[]{:S(2)}, u32[]{:S(2)}) %collective-permute-start.4) | collective-permute-done | bytes 442400 | tf_op jit(solution)/shard_map/ppermute | solution.py:35
  113.8 2.3 shard_map.91
  123.5 10.0 %collective-permute-start.36 = (bf16[16,3456]{1,0:T(8,128)(2,1)S(1)}, bf16[16,3456]{1,0:T(8,128)(2,1)S(1)}, u32[]{:S(2)}, u32[]{:S(2)}) collective-permute-start(bf16[16,3456]{1,0:T(8,128)(2,1)S(1)} %copy.156), channel_id=1, source_target_pairs={{0,8},{2,10},{4,12},{6,14},{8,0},{10,2},{12,4},{14,6},{16,24},{18,... | collective-permute-start | bytes 331784 | tf_op jit(solution)/shard_map/ppermute | solution.py:35
  145.1 6.6 %shard_map.94 = bf16[2,17,320,128]{3,2,1,0:T(8,128)(2,1)S(1)} custom-call(s32[2]{0:T(128)S(1)} %pad_add_fusion.where.refs_0_, bf16[128,1280]{1,0:T(8,128)(2,1)S(1)} %copy-done.5, bf16[640,1280]{1,0:T(8,128)(2,1)S(1)} %select_bitcast_fusion.refs_2_, bf16[16,64,1280]{2,1,0:T(8,128)(2,1)S(1)} %copy-done.6, bf16[16,64,1280]{2,1,0:T(8,128)(2,1)} %collective-permute-done.24.refs_4_), custom_call_target="tpu_custom_call" | custom-call | flops 3565158400 | bytes 12124160 | tf_op jit(solution)/shard_map/pallas_call | solution.py:149
  151.7 2.5 dynamic-slice_bitcast_fusion.2
  157.4 9.6 %collective-permute-start.37 = (bf16[16,3456]{1,0:T(8,128)(2,1)S(1)}, bf16[16,3456]{1,0:T(8,128)(2,1)S(1)}, u32[]{:S(2)}, u32[]{:S(2)}) collective-permute-start(bf16[16,3456]{1,0:T(8,128)(2,1)S(1)} %copy.158), channel_id=1, source_target_pairs={{0,16},{2,18},{4,20},{6,22},{8,24},{10,26},{12,28},{14,30},{16,0},... | collective-permute-start | bytes 331784 | tf_op jit(solution)/shard_map/ppermute | solution.py:35
  167.0 5.5 %collective-permute-done.37 = bf16[16,3456]{1,0:T(8,128)(2,1)S(1)} collective-permute-done((bf16[16,3456]{1,0:T(8,128)(2,1)S(1)}, bf16[16,3456]{1,0:T(8,128)(2,1)S(1)}, u32[]{:S(2)}, u32[]{:S(2)}) %collective-permute-start.37) | collective-permute-done | bytes 110624 | tf_op jit(solution)/shard_map/ppermute | solution.py:35
  176.9 2.5 collective-permute-start.32
  186.4 7.2 %shard_map.92 = (bf16[2,2,864,128]{3,2,1,0:T(8,128)(2,1)S(1)}, bf16[2,2,864,128]{3,2,1,0:T(8,128)(2,1)S(1)}, bf16[2,2,864,128]{3,2,1,0:T(8,128)(2,1)S(1)}, bf16[2,2,864,128]{3,2,1,0:T(8,128)(2,1)S(1)}) custom-call(s32[2]{0:T(128)S(1)} %pad_add_fusion.where.refs_0_, bf16[4,864,864]{2,1,0:T(8,128)(2,1)S(1)} %bitcast.201, bf16[16,64,864]{2,1,0:T(8,128)(2,1)S(1)} %copy-done.7, ...), custom_call_target="tpu_custom_call" | custom-call | flops 3057647616 | bytes 10395648 | tf_op jit(solution)/shard_map/pallas_call | solution.py:201
  197.3 7.8 %collective-permute-done.32.refs_2_ = bf16[1,320,864]{2,1,0:T(8,128)(2,1)S(1)} collective-permute-done((bf16[1,320,864]{2,1,0:T(8,128)(2,1)S(1)}, bf16[1,320,864]{2,1,0:T(8,128)(2,1)S(1)}, u32[]{:S(2)}, u32[]{:S(2)}) %collective-permute-start.32) | collective-permute-done | bytes 552992 | tf_op jit(solution)/shard_map/ppermute | solution.py:35
  209.8 7.2 %shard_map.105 = (bf16[2,2,864,128]{3,2,1,0:T(8,128)(2,1)S(1)}, bf16[2,2,864,128]{3,2,1,0:T(8,128)(2,1)S(1)}, bf16[2,2,864,128]{3,2,1,0:T(8,128)(2,1)S(1)}, bf16[2,2,864,128]{3,2,1,0:T(8,128)(2,1)S(1)}) custom-call(s32[2]{0:T(128)S(1)} %pad_add_fusion.where.refs_0_, bf16[4,864,864]{2,1,0:T(8,128)(2,1)S(1)} %bitcast.202, bf16[16,64,864]{2,1,0:T(8,128)(2,1)S(1)} %copy-done.7, ...), custom_call_target="tpu_custom_call" | custom-call | flops 3057647616 | bytes 10395648 | tf_op jit(solution)/shard_map/pallas_call | solution.py:201
  217.0 7.3 %shard_map.102 = (bf16[2,2,864,128]{3,2,1,0:T(8,128)(2,1)S(1)}, bf16[2,2,864,128]{3,2,1,0:T(8,128)(2,1)S(1)}, bf16[2,2,864,128]{3,2,1,0:T(8,128)(2,1)S(1)}, bf16[2,2,864,128]{3,2,1,0:T(8,128)(2,1)S(1)}) custom-call(s32[2]{0:T(128)S(1)} %pad_add_fusion.where.refs_0_, bf16[4,864,864]{2,1,0:T(8,128)(2,1)S(1)} %bitcast.203, bf16[16,64,864]{2,1,0:T(8,128)(2,1)S(1)} %copy-done.7, ...), custom_call_target="tpu_custom_call" | custom-call | flops 3057647616 | bytes 10395648 | tf_op jit(solution)/shard_map/pallas_call | solution.py:201
  224.3 7.2 %shard_map.99 = (bf16[2,2,864,128]{3,2,1,0:T(8,128)(2,1)S(1)}, bf16[2,2,864,128]{3,2,1,0:T(8,128)(2,1)S(1)}, bf16[2,2,864,128]{3,2,1,0:T(8,128)(2,1)S(1)}, bf16[2,2,864,128]{3,2,1,0:T(8,128)(2,1)S(1)}) custom-call(s32[2]{0:T(128)S(1)} %pad_add_fusion.where.refs_0_, bf16[4,864,864]{2,1,0:T(8,128)(2,1)S(1)} %bitcast.204, bf16[16,64,864]{2,1,0:T(8,128)(2,1)S(1)} %copy-done.7, ...), custom_call_target="tpu_custom_call" | custom-call | flops 3057647616 | bytes 10395648 | tf_op jit(solution)/shard_map/pallas_call | solution.py:201
  240.5 13.7 %collective-permute-done.43 = bf16[2,2,864,128]{3,2,1,0:T(8,128)(2,1)S(1)} collective-permute-done((bf16[2,2,864,128]{3,2,1,0:T(8,128)(2,1)S(1)}, bf16[2,2,864,128]{3,2,1,0:T(8,128)(2,1)S(1)}, u32[]{:S(2)}, u32[]{:S(2)}) %collective-permute-start.43) | collective-permute-done | bytes 884768 | tf_op jit(solution)/shard_map/ppermute | solution.py:35
  256.6 8.8 %collective-permute-done.27 = bf16[1,17,160,128]{3,2,1,0:T(8,128)(2,1)S(1)} collective-permute-done((bf16[1,17,160,128]{3,2,1,0:T(8,128)(2,1)S(1)}, bf16[1,17,160,128]{3,2,1,0:T(8,128)(2,1)S(1)}, u32[]{:S(2)}, u32[]{:S(2)}) %collective-permute-start.27) | collective-permute-done | bytes 696352 | tf_op jit(solution)/shard_map/ppermute | solution.py:35
  265.6 2.8 collective-permute-start.40
  271.5 13.6 %collective-permute-done.40 = bf16[17,160,128]{2,1,0:T(8,128)(2,1)S(1)} collective-permute-done((bf16[17,160,128]{2,1,0:T(8,128)(2,1)S(1)}, bf16[17,160,128]{2,1,0:T(8,128)(2,1)S(1)}, u32[]{:S(2)}, u32[]{:S(2)}) %collective-permute-start.40) | collective-permute-done | bytes 696352 | tf_op jit(solution)/shard_map/ppermute | solution.py:35
  285.9 13.3 %collective-permute-done.39 = bf16[17,160,128]{2,1,0:T(8,128)(2,1)S(1)} collective-permute-done((bf16[17,160,128]{2,1,0:T(8,128)(2,1)S(1)}, bf16[17,160,128]{2,1,0:T(8,128)(2,1)S(1)}, u32[]{:S(2)}, u32[]{:S(2)}) %collective-permute-start.39) | collective-permute-done | bytes 696352 | tf_op jit(solution)/shard_map/ppermute | solution.py:35
  304.5 4.1 collective-permute-done.11
  310.2 17.3 %collective-permute-done.53 = bf16[2,2,864,128]{3,2,1,0:T(8,128)(2,1)S(1)} collective-permute-done((bf16[2,2,864,128]{3,2,1,0:T(8,128)(2,1)S(1)}, bf16[2,2,864,128]{3,2,1,0:T(8,128)(2,1)S(1)}, u32[]{:S(2)}, u32[]{:S(2)}) %collective-permute-start.53) | collective-permute-done | bytes 884768 | tf_op jit(solution)/shard_map/ppermute | solution.py:35
  331.8 8.1 %collective-permute-done.54 = bf16[2,864,128]{2,1,0:T(8,128)(2,1)S(1)} collective-permute-done((bf16[2,864,128]{2,1,0:T(8,128)(2,1)S(1)}, bf16[2,864,128]{2,1,0:T(8,128)(2,1)S(1)}, u32[]{:S(2)}, u32[]{:S(2)}) %collective-permute-start.54) | collective-permute-done | bytes 442400 | tf_op jit(solution)/shard_map/ppermute | solution.py:35
  342.9 4.5 collective-permute-done.28
  347.6 12.5 %collective-permute-done.61 = bf16[2,2,864,128]{3,2,1,0:T(8,128)(2,1)S(1)} collective-permute-done((bf16[2,2,864,128]{3,2,1,0:T(8,128)(2,1)S(1)}, bf16[2,2,864,128]{3,2,1,0:T(8,128)(2,1)S(1)}, u32[]{:S(2)}, u32[]{:S(2)}) %collective-permute-start.61) | collective-permute-done | bytes 884768 | tf_op jit(solution)/shard_map/ppermute | solution.py:35
  362.8 15.3 %collective-permute-done.56 = bf16[1,864,128]{2,1,0:T(8,128)(2,1)S(1)} collective-permute-done((bf16[1,864,128]{2,1,0:T(8,128)(2,1)S(1)}, bf16[1,864,128]{2,1,0:T(8,128)(2,1)S(1)}, u32[]{:S(2)}, u32[]{:S(2)}) %collective-permute-start.56) | collective-permute-done | bytes 221216 | tf_op jit(solution)/shard_map/ppermute | solution.py:35
  378.4 9.4 %collective-permute-done.60 = bf16[2,864,128]{2,1,0:T(8,128)(2,1)S(1)} collective-permute-done((bf16[2,864,128]{2,1,0:T(8,128)(2,1)S(1)}, bf16[2,864,128]{2,1,0:T(8,128)(2,1)S(1)}, u32[]{:S(2)}, u32[]{:S(2)}) %collective-permute-start.60) | collective-permute-done | bytes 442400 | tf_op jit(solution)/shard_map/ppermute | solution.py:35
  390.6 12.9 %collective-permute-done.30 = bf16[1,864,128]{2,1,0:T(8,128)(2,1)S(1)} collective-permute-done((bf16[1,864,128]{2,1,0:T(8,128)(2,1)S(1)}, bf16[1,864,128]{2,1,0:T(8,128)(2,1)S(1)}, u32[]{:S(2)}, u32[]{:S(2)}) %collective-permute-start.30) | collective-permute-done | bytes 221216 | tf_op jit(solution)/shard_map/ppermute | solution.py:35
  407.3 20.1 %collective-permute-done.58.b_ref = bf16[2,864,128]{2,1,0:T(8,128)(2,1)S(1)} collective-permute-done((bf16[2,864,128]{2,1,0:T(8,128)(2,1)S(1)}, bf16[2,864,128]{2,1,0:T(8,128)(2,1)S(1)}, u32[]{:S(2)}, u32[]{:S(2)}) %collective-permute-start.58) | collective-permute-done | bytes 442400 | tf_op jit(solution)/shard_map/ppermute | solution.py:35
  428.9 8.5 %shard_map.104 = f32[2,2,128]{2,1,0:T(2,128)S(1)} custom-call(s32[2]{0:T(128)S(1)} %pad_add_fusion.where.refs_0_, bf16[2,864,128]{2,1,0:T(8,128)(2,1)S(1)} %collective-permute-done.58.b_ref, f32[864,1280]{1,0:T(8,128)} %copy-done, f32[864,128]{1,0:T(8,128)S(1)} %convert_bitcast_fusion.query_b, f32[16,1,128]{2,1,0:T(1,128)S(1)} %bitcast.206, ...), custom_call_target="tpu_custom_call" | custom-call | flops 9059696640 | bytes 10436608 | tf_op jit(solution)/shard_map/pallas_call | solution.py:261
  437.4 8.6 %shard_map.103 = f32[2,2,128]{2,1,0:T(2,128)S(1)} custom-call(s32[2]{0:T(128)S(1)} %pad_add_fusion.where.refs_0_, bf16[2,864,128]{2,1,0:T(8,128)(2,1)S(1)} %pad_maximum_fusion.12.b_ref, f32[864,1280]{1,0:T(8,128)} %copy-done, f32[864,128]{1,0:T(8,128)S(1)} %convert_bitcast_fusion.query_b, f32[16,1,128]{2,1,0:T(1,128)S(1)} %bitcast.207, ...), custom_call_target="tpu_custom_call" | custom-call | flops 9059696640 | bytes 10436608 | tf_op jit(solution)/shard_map/pallas_call | solution.py:261
  446.1 8.5 %shard_map.101 = f32[2,2,128]{2,1,0:T(2,128)S(1)} custom-call(s32[2]{0:T(128)S(1)} %pad_add_fusion.where.refs_0_, bf16[2,864,128]{2,1,0:T(8,128)(2,1)S(1)} %collective-permute-done.50.b_ref, f32[864,1280]{1,0:T(8,128)} %copy-done, f32[864,128]{1,0:T(8,128)S(1)} %convert_bitcast_fusion.query_b, f32[16,1,128]{2,1,0:T(1,128)S(1)} %bitcast.208, ...), custom_call_target="tpu_custom_call" | custom-call | flops 9059696640 | bytes 10436608 | tf_op jit(solution)/shard_map/pallas_call | solution.py:261
  454.6 8.4 %shard_map.100 = f32[2,2,128]{2,1,0:T(2,128)S(1)} custom-call(s32[2]{0:T(128)S(1)} %pad_add_fusion.where.refs_0_, bf16[2,864,128]{2,1,0:T(8,128)(2,1)S(1)} %pad_maximum_fusion.11.b_ref, f32[864,1280]{1,0:T(8,128)} %copy-done, f32[864,128]{1,0:T(8,128)S(1)} %convert_bitcast_fusion.query_b, f32[16,1,128]{2,1,0:T(1,128)S(1)} %bitcast.209, ...), custom_call_target="tpu_custom_call" | custom-call | flops 9059696640 | bytes 10436608 | tf_op jit(solution)/shard_map/pallas_call | solution.py:261
  463.2 8.7 %shard_map.98 = f32[2,2,128]{2,1,0:T(2,128)S(1)} custom-call(s32[2]{0:T(128)S(1)} %pad_add_fusion.where.refs_0_, bf16[2,864,128]{2,1,0:T(8,128)(2,1)S(1)} %collective-permute-done.42.b_ref, f32[864,1280]{1,0:T(8,128)} %copy-done, f32[864,128]{1,0:T(8,128)S(1)} %convert_bitcast_fusion.query_b, f32[16,1,128]{2,1,0:T(1,128)S(1)} %bitcast.210, ...), custom_call_target="tpu_custom_call" | custom-call | flops 9059696640 | bytes 10436608 | tf_op jit(solution)/shard_map/pallas_call | solution.py:261
  471.9 8.4 %shard_map.97 = f32[2,2,128]{2,1,0:T(2,128)S(1)} custom-call(s32[2]{0:T(128)S(1)} %pad_add_fusion.where.refs_0_, bf16[2,864,128]{2,1,0:T(8,128)(2,1)S(1)} %pad_maximum_fusion.10.b_ref, f32[864,1280]{1,0:T(8,128)} %copy-done, f32[864,128]{1,0:T(8,128)S(1)} %convert_bitcast_fusion.query_b, f32[16,1,128]{2,1,0:T(1,128)S(1)} %bitcast.211, ...), custom_call_target="tpu_custom_call" | custom-call | flops 9059696640 | bytes 10436608 | tf_op jit(solution)/shard_map/pallas_call | solution.py:261
  480.7 8.3 %collective-permute-done.65 = bf16[1,864,128]{2,1,0:T(8,128)(2,1)S(1)} collective-permute-done((bf16[1,864,128]{2,1,0:T(8,128)(2,1)S(1)}, bf16[1,864,128]{2,1,0:T(8,128)(2,1)S(1)}, u32[]{:S(2)}, u32[]{:S(2)}) %collective-permute-start.65) | collective-permute-done | bytes 221216 | tf_op jit(solution)/shard_map/ppermute | solution.py:35
  489.1 8.7 %shard_map.106 = f32[2,2,128]{2,1,0:T(2,128)S(1)} custom-call(s32[2]{0:T(128)S(1)} %pad_add_fusion.where.refs_0_, bf16[2,864,128]{2,1,0:T(8,128)(2,1)S(1)} %pad_maximum_fusion.13.b_ref, f32[864,1280]{1,0:T(8,128)} %copy-done, f32[864,128]{1,0:T(8,128)S(1)} %convert_bitcast_fusion.query_b, f32[16,1,128]{2,1,0:T(1,128)S(1)} %bitcast.212, ...), custom_call_target="tpu_custom_call" | custom-call | flops 9059696640 | bytes 10436608 | tf_op jit(solution)/shard_map/pallas_call | solution.py:261
  498.3 8.5 %shard_map.107 = f32[2,2,128]{2,1,0:T(2,128)S(1)} custom-call(s32[2]{0:T(128)S(1)} %pad_add_fusion.where.refs_0_, bf16[2,864,128]{2,1,0:T(8,128)(2,1)S(1)} %collective-permute-done.66.b_ref, f32[864,1280]{1,0:T(8,128)} %copy-done, f32[864,128]{1,0:T(8,128)S(1)} %convert_bitcast_fusion.query_b, f32[16,1,128]{2,1,0:T(1,128)S(1)} %bitcast.213, ...), custom_call_target="tpu_custom_call" | custom-call | flops 9059696640 | bytes 10436608 | tf_op jit(solution)/shard_map/pallas_call | solution.py:261
  507.1 14.6 %all_to_all.5 = f32[16,2,16]{2,1,0:T(2,128)S(1)} all-to-all(f32[16,2,16]{2,1,0:T(2,128)S(1)} %multiply_reduce_fusion), channel_id=1, replica_groups=mesh['seq'=16,'eig'=2] {'seq'}, dimensions={0} | all-to-all | bytes 4096 | tf_op jit(solution)/shard_map/all_to_all | solution.py:445
  (316 shorter events, 142.9 us)
Async XLA Ops:
  2.2 22.7 %collective-permute-start.14 = (bf16[1,1,19073]{2,0,1:T(2,128)(2,1)S(1)}, bf16[1,1,19073]{2,0,1:T(2,128)(2,1)S(1)}, u32[]{:S(2)}, u32[]{:S(2)}) collective-permute-start(bf16[1,1,19073]{2,0,1:T(2,128)(2,1)S(1)} %maximum_bitcast_fusion.2), channel_id=1, source_target_pairs={{0,8},{2,10},{4,12},{6,14},{8,0},{10,2},{12,4},{14,6},{16,24},{18,... | collective-permute-start | bytes 114446 | tf_op jit(solution)/shard_map/ppermute | solution.py:35
  7.3 25.7 %collective-permute-start = (bf16[64,1280]{1,0:T(8,128)(2,1)}, bf16[64,1280]{1,0:T(8,128)(2,1)S(1)}, u32[]{:S(2)}, u32[]{:S(2)}) collective-permute-start(bf16[64,1280]{1,0:T(8,128)(2,1)} %get-tuple-element.104), channel_id=1, source_target_pairs={{0,8},{2,10},{4,12},{6,14},{8,0},{10,2},{12,4},{14,6},{16,24},{18,... | collective-permute-start | bytes 491528 | tf_op jit(solution)/shard_map/ppermute | solution.py:35
  7.4 26.2 %collective-permute-start.1 = (bf16[64,1280]{1,0:T(8,128)(2,1)}, bf16[64,1280]{1,0:T(8,128)(2,1)}, u32[]{:S(2)}, u32[]{:S(2)}) collective-permute-start(bf16[64,1280]{1,0:T(8,128)(2,1)} %get-tuple-element.103), channel_id=1, source_target_pairs={{0,16},{2,18},{4,20},{6,22},{8,24},{10,26},{12,28},{14,30},{16,0},... | collective-permute-start | bytes 491528 | tf_op jit(solution)/shard_map/ppermute | solution.py:35
  10.4 24.7 %collective-permute-start.2 = (bf16[64,1280]{1,0:T(8,128)(2,1)}, bf16[64,1280]{1,0:T(8,128)(2,1)}, u32[]{:S(2)}, u32[]{:S(2)}) collective-permute-start(bf16[64,1280]{1,0:T(8,128)(2,1)} %get-tuple-element.105), channel_id=1, source_target_pairs={{0,24},{2,26},{4,28},{6,30},{8,16},{10,18},{12,20},{14,22},{16,8},... | collective-permute-start | bytes 491528 | tf_op jit(solution)/shard_map/ppermute | solution.py:35
  14.2 33.6 %collective-permute-start.18 = (bf16[1,320,640]{2,1,0:T(8,128)(2,1)S(1)}, bf16[1,320,640]{2,1,0:T(8,128)(2,1)S(1)}, u32[]{:S(2)}, u32[]{:S(2)}) collective-permute-start(bf16[1,320,640]{2,1,0:T(8,128)(2,1)S(1)} %get-tuple-element.56), channel_id=1, source_target_pairs={{0,2},{2,0},{4,6},{6,4},{8,10},{10,8},{12,14},{14,12},{16,18},{18,... | collective-permute-start | bytes 1228808 | tf_op jit(solution)/shard_map/ppermute | solution.py:35
  31.1 20.5 %collective-permute-start.19 = (bf16[1,320,640]{2,1,0:T(8,128)(2,1)S(1)}, bf16[1,320,640]{2,1,0:T(8,128)(2,1)S(1)}, u32[]{:S(2)}, u32[]{:S(2)}) collective-permute-start(bf16[1,320,640]{2,1,0:T(8,128)(2,1)S(1)} %get-tuple-element.57), channel_id=1, source_target_pairs={{0,4},{2,6},{4,0},{6,2},{8,12},{10,14},{12,8},{14,10},{16,20},{18,... | collective-permute-start | bytes 1228808 | tf_op jit(solution)/shard_map/ppermute | solution.py:35
  33.1 18.6 %collective-permute-start.20 = (bf16[1,320,640]{2,1,0:T(8,128)(2,1)S(1)}, bf16[1,320,640]{2,1,0:T(8,128)(2,1)S(1)}, u32[]{:S(2)}, u32[]{:S(2)}) collective-permute-start(bf16[1,320,640]{2,1,0:T(8,128)(2,1)S(1)} %get-tuple-element.58), channel_id=1, source_target_pairs={{0,6},{2,4},{4,2},{6,0},{8,14},{10,12},{12,10},{14,8},{16,22},{18,... | collective-permute-start | bytes 1228808 | tf_op jit(solution)/shard_map/ppermute | solution.py:35
  37.6 63.7 %collective-permute-start.3 = (bf16[64,3456]{1,0:T(8,128)(2,1)}, bf16[64,3456]{1,0:T(8,128)(2,1)S(1)}, u32[]{:S(2)}, u32[]{:S(2)}) collective-permute-start(bf16[64,3456]{1,0:T(8,128)(2,1)} %get-tuple-element.89), channel_id=1, source_target_pairs={{0,8},{2,10},{4,12},{6,14},{8,0},{10,2},{12,4},{14,6},{16,24},{18,... | collective-permute-start | bytes 1327112 | tf_op jit(solution)/shard_map/ppermute | solution.py:35
  46.3 27.0 %collective-permute-start.17 = (bf16[4,2,1,19073]{3,0,2,1:T(4,128)(2,1)}, bf16[4,2,1,19073]{3,0,2,1:T(4,128)(2,1)}, u32[]{:S(2)}, u32[]{:S(2)}) collective-permute-start(bf16[4,2,1,19073]{3,0,2,1:T(4,128)(2,1)} %pad_maximum_fusion.14), channel_id=1, source_target_pairs={{0,4},{2,6},{4,0},{6,2},{8,12},{10,14},{12,8},{14,10},{16,20},{18,... | collective-permute-start | bytes 915512 | tf_op jit(solution)/shard_map/ppermute | solution.py:35
  51.6 37.1 %collective-permute-start.21 = (bf16[4,64,1280]{2,1,0:T(8,128)(2,1)}, bf16[4,64,1280]{2,1,0:T(8,128)(2,1)}, u32[]{:S(2)}, u32[]{:S(2)}) collective-permute-start(bf16[4,64,1280]{2,1,0:T(8,128)(2,1)} %pad_maximum_fusion.8), channel_id=1, source_target_pairs={{0,2},{2,0},{4,6},{6,4},{8,10},{10,8},{12,14},{14,12},{16,18},{18,... | collective-permute-start | bytes 1966088 | tf_op jit(solution)/shard_map/ppermute | solution.py:35
  52.2 40.1 %collective-permute-start.22 = (bf16[4,64,1280]{2,1,0:T(8,128)(2,1)}, bf16[4,64,1280]{2,1,0:T(8,128)(2,1)}, u32[]{:S(2)}, u32[]{:S(2)}) collective-permute-start(bf16[4,64,1280]{2,1,0:T(8,128)(2,1)} %pad_maximum_fusion.8), channel_id=1, source_target_pairs={{0,4},{2,6},{4,0},{6,2},{8,12},{10,14},{12,8},{14,10},{16,20},{18,... | collective-permute-start | bytes 1966088 | tf_op jit(solution)/shard_map/ppermute | solution.py:35
  52.7 41.6 %collective-permute-start.23 = (bf16[4,64,1280]{2,1,0:T(8,128)(2,1)}, bf16[4,64,1280]{2,1,0:T(8,128)(2,1)}, u32[]{:S(2)}, u32[]{:S(2)}) collective-permute-start(bf16[4,64,1280]{2,1,0:T(8,128)(2,1)} %pad_maximum_fusion.8), channel_id=1, source_target_pairs={{0,6},{2,4},{4,2},{6,0},{8,14},{10,12},{12,10},{14,8},{16,22},{18,... | collective-permute-start | bytes 1966088 | tf_op jit(solution)/shard_map/ppermute | solution.py:35
  86.2 25.8 %collective-permute-start.4 = (bf16[64,3456]{1,0:T(8,128)(2,1)}, bf16[64,3456]{1,0:T(8,128)(2,1)S(1)}, u32[]{:S(2)}, u32[]{:S(2)}) collective-permute-start(bf16[64,3456]{1,0:T(8,128)(2,1)} %get-tuple-element.88), channel_id=1, source_target_pairs={{0,16},{2,18},{4,20},{6,22},{8,24},{10,26},{12,28},{14,30},{16,0},... | collective-permute-start | bytes 1327112 | tf_op jit(solution)/shard_map/ppermute | solution.py:35
  88.8 23.2 %collective-permute-start.5 = (bf16[64,3456]{1,0:T(8,128)(2,1)}, bf16[64,3456]{1,0:T(8,128)(2,1)S(1)}, u32[]{:S(2)}, u32[]{:S(2)}) collective-permute-start(bf16[64,3456]{1,0:T(8,128)(2,1)} %get-tuple-element.87), channel_id=1, source_target_pairs={{0,24},{2,26},{4,28},{6,30},{8,16},{10,18},{12,20},{14,22},{16,8},... | collective-permute-start | bytes 1327112 | tf_op jit(solution)/shard_map/ppermute | solution.py:35
  96.3 47.1 %collective-permute-start.24 = (bf16[16,64,1280]{2,1,0:T(8,128)(2,1)}, bf16[16,64,1280]{2,1,0:T(8,128)(2,1)}, u32[]{:S(2)}, u32[]{:S(2)}) collective-permute-start(bf16[16,64,1280]{2,1,0:T(8,128)(2,1)} %constant_dynamic-update-slice_fusion.8.refs_3_), channel_id=1, source_target_pairs={{0,1},{1,0},{2,3},{3,2},{4,5},{5,4},{6,7},{7,6},{8,9},{9,8},{10,11... | collective-permute-start | bytes 7864328 | tf_op jit(solution)/shard_map/ppermute | solution.py:35
  99.5 20.3 %collective-permute-start.35 = (bf16[16,3456]{1,0:T(8,128)(2,1)}, bf16[16,3456]{1,0:T(8,128)(2,1)S(1)}, u32[]{:S(2)}, u32[]{:S(2)}) collective-permute-start(bf16[16,3456]{1,0:T(8,128)(2,1)} %copy.154), channel_id=1, source_target_pairs={{0,4},{2,6},{4,0},{6,2},{8,12},{10,14},{12,8},{14,10},{16,20},{18,... | collective-permute-start | bytes 331784 | tf_op jit(solution)/shard_map/ppermute | solution.py:35
  116.1 21.7 %collective-permute-start.6 = (bf16[4,64,864]{2,1,0:T(8,128)(2,1)}, bf16[4,64,864]{2,1,0:T(8,128)(2,1)}, u32[]{:S(2)}, u32[]{:S(2)}) collective-permute-start(bf16[4,64,864]{2,1,0:T(8,128)(2,1)} %get-tuple-element.48), channel_id=1, source_target_pairs={{0,2},{2,0},{4,6},{6,4},{8,10},{10,8},{12,14},{14,12},{16,18},{18,... | collective-permute-start | bytes 1327112 | tf_op jit(solution)/shard_map/ppermute | solution.py:35
  116.6 23.0 %collective-permute-start.7 = (bf16[4,64,864]{2,1,0:T(8,128)(2,1)}, bf16[4,64,864]{2,1,0:T(8,128)(2,1)}, u32[]{:S(2)}, u32[]{:S(2)}) collective-permute-start(bf16[4,64,864]{2,1,0:T(8,128)(2,1)} %get-tuple-element.49), channel_id=1, source_target_pairs={{0,4},{2,6},{4,0},{6,2},{8,12},{10,14},{12,8},{14,10},{16,20},{18,... | collective-permute-start | bytes 1327112 | tf_op jit(solution)/shard_map/ppermute | solution.py:35
  118.9 22.7 %collective-permute-start.8 = (bf16[4,64,864]{2,1,0:T(8,128)(2,1)}, bf16[4,64,864]{2,1,0:T(8,128)(2,1)}, u32[]{:S(2)}, u32[]{:S(2)}) collective-permute-start(bf16[4,64,864]{2,1,0:T(8,128)(2,1)} %get-tuple-element.50), channel_id=1, source_target_pairs={{0,6},{2,4},{4,2},{6,0},{8,14},{10,12},{12,10},{14,8},{16,22},{18,... | collective-permute-start | bytes 1327112 | tf_op jit(solution)/shard_map/ppermute | solution.py:35
  143.4 41.3 %collective-permute-start.9 = (bf16[16,64,864]{2,1,0:T(8,128)(2,1)}, bf16[16,64,864]{2,1,0:T(8,128)(2,1)}, u32[]{:S(2)}, u32[]{:S(2)}) collective-permute-start(bf16[16,64,864]{2,1,0:T(8,128)(2,1)} %constant_dynamic-update-slice_fusion.refs_0_), channel_id=1, source_target_pairs={{0,1},{1,0},{2,3},{3,2},{4,5},{5,4},{6,7},{7,6},{8,9},{9,8},{10,11... | collective-permute-start | bytes 5308424 | tf_op jit(solution)/shard_map/ppermute | solution.py:35
  154.2 25.2 %collective-permute-start.25 = (bf16[2,17,160,128]{3,2,1,0:T(8,128)(2,1)}, bf16[2,17,160,128]{3,2,1,0:T(8,128)(2,1)}, u32[]{:S(2)}, u32[]{:S(2)}) collective-permute-start(bf16[2,17,160,128]{3,2,1,0:T(8,128)(2,1)} %get-tuple-element.95), channel_id=1, source_target_pairs={{0,1},{1,0},{2,3},{3,2},{4,5},{5,4},{6,7},{7,6},{8,9},{9,8},{10,11... | collective-permute-start | bytes 4177928 | tf_op jit(solution)/shard_map/ppermute | solution.py:35
  175.3 19.9 %collective-permute-start.31 = (bf16[1,320,864]{2,1,0:T(8,128)(2,1)S(1)}, bf16[1,320,864]{2,1,0:T(8,128)(2,1)S(1)}, u32[]{:S(2)}, u32[]{:S(2)}) collective-permute-start(bf16[1,320,864]{2,1,0:T(8,128)(2,1)S(1)} %get-tuple-element.63), channel_id=1, source_target_pairs={{0,2},{2,0},{4,6},{6,4},{8,10},{10,8},{12,14},{14,12},{16,18},{18,... | collective-permute-start | bytes 1658888 | tf_op jit(solution)/shard_map/ppermute | solution.py:35
  176.9 28.2 %collective-permute-start.32 = (bf16[1,320,864]{2,1,0:T(8,128)(2,1)S(1)}, bf16[1,320,864]{2,1,0:T(8,128)(2,1)S(1)}, u32[]{:S(2)}, u32[]{:S(2)}) collective-permute-start(bf16[1,320,864]{2,1,0:T(8,128)(2,1)S(1)} %get-tuple-element.64), channel_id=1, source_target_pairs={{0,4},{2,6},{4,0},{6,2},{8,12},{10,14},{12,8},{14,10},{16,20},{18,... | collective-permute-start | bytes 1658888 | tf_op jit(solution)/shard_map/ppermute | solution.py:35
  179.4 26.2 %collective-permute-start.33 = (bf16[1,320,864]{2,1,0:T(8,128)(2,1)S(1)}, bf16[1,320,864]{2,1,0:T(8,128)(2,1)S(1)}, u32[]{:S(2)}, u32[]{:S(2)}) collective-permute-start(bf16[1,320,864]{2,1,0:T(8,128)(2,1)S(1)} %get-tuple-element.65), channel_id=1, source_target_pairs={{0,6},{2,4},{4,2},{6,0},{8,14},{10,12},{12,10},{14,8},{16,22},{18,... | collective-permute-start | bytes 1658888 | tf_op jit(solution)/shard_map/ppermute | solution.py:35
  184.6 52.2 %collective-permute-start.26 = (bf16[2,17,160,128]{3,2,1,0:T(8,128)(2,1)}, bf16[2,17,160,128]{3,2,1,0:T(8,128)(2,1)}, u32[]{:S(2)}, u32[]{:S(2)}) collective-permute-start(bf16[2,17,160,128]{3,2,1,0:T(8,128)(2,1)} %dynamic-slice_bitcast_fusion), channel_id=1, source_target_pairs={{0,8},{2,10},{4,12},{6,14},{8,0},{10,2},{12,4},{14,6},{16,24},{18,... | collective-permute-start | bytes 4177928 | tf_op jit(solution)/shard_map/ppermute | solution.py:35
  193.7 37.9 %collective-permute-start.10 = (bf16[2,2,864,128]{3,2,1,0:T(8,128)(2,1)S(1)}, bf16[2,2,864,128]{3,2,1,0:T(8,128)(2,1)}, u32[]{:S(2)}, u32[]{:S(2)}) collective-permute-start(bf16[2,2,864,128]{3,2,1,0:T(8,128)(2,1)S(1)} %get-tuple-element.52), channel_id=1, source_target_pairs={{0,2},{2,0},{4,6},{6,4},{8,10},{10,8},{12,14},{14,12},{16,18},{18,... | collective-permute-start | bytes 2654216 | tf_op jit(solution)/shard_map/ppermute | solution.py:35
  195.2 36.3 %collective-permute-start.12 = (bf16[2,2,864,128]{3,2,1,0:T(8,128)(2,1)S(1)}, bf16[2,2,864,128]{3,2,1,0:T(8,128)(2,1)}, u32[]{:S(2)}, u32[]{:S(2)}) collective-permute-start(bf16[2,2,864,128]{3,2,1,0:T(8,128)(2,1)S(1)} %get-tuple-element.54), channel_id=1, source_target_pairs={{0,4},{2,6},{4,0},{6,2},{8,12},{10,14},{12,8},{14,10},{16,20},{18,... | collective-permute-start | bytes 2654216 | tf_op jit(solution)/shard_map/ppermute | solution.py:35
  231.6 22.7 %collective-permute-start.43 = (bf16[2,2,864,128]{3,2,1,0:T(8,128)(2,1)S(1)}, bf16[2,2,864,128]{3,2,1,0:T(8,128)(2,1)S(1)}, u32[]{:S(2)}, u32[]{:S(2)}) collective-permute-start(bf16[2,2,864,128]{3,2,1,0:T(8,128)(2,1)S(1)} %get-tuple-element.70), channel_id=1, source_target_pairs={{0,2},{2,0},{4,6},{6,4},{8,10},{10,8},{12,14},{14,12},{16,18},{18,... | collective-permute-start | bytes 2654216 | tf_op jit(solution)/shard_map/ppermute | solution.py:35
  233.1 21.1 %collective-permute-start.45 = (bf16[2,2,864,128]{3,2,1,0:T(8,128)(2,1)S(1)}, bf16[2,2,864,128]{3,2,1,0:T(8,128)(2,1)S(1)}, u32[]{:S(2)}, u32[]{:S(2)}) collective-permute-start(bf16[2,2,864,128]{3,2,1,0:T(8,128)(2,1)S(1)} %get-tuple-element.72), channel_id=1, source_target_pairs={{0,4},{2,6},{4,0},{6,2},{8,12},{10,14},{12,8},{14,10},{16,20},{18,... | collective-permute-start | bytes 2654216 | tf_op jit(solution)/shard_map/ppermute | solution.py:35
  234.9 66.9 %collective-permute-start.13 = (bf16[2,864,128]{2,1,0:T(8,128)(2,1)S(1)}, bf16[2,864,128]{2,1,0:T(8,128)(2,1)S(1)}, u32[]{:S(2)}, u32[]{:S(2)}) collective-permute-start(bf16[2,864,128]{2,1,0:T(8,128)(2,1)S(1)} %fusion.15), channel_id=1, source_target_pairs={{0,2},{2,0},{4,6},{6,4},{8,10},{10,8},{12,14},{14,12},{16,18},{18,... | collective-permute-start | bytes 1327112 | tf_op jit(solution)/shard_map/ppermute | solution.py:35
  239.1 26.4 %collective-permute-start.27 = (bf16[1,17,160,128]{3,2,1,0:T(8,128)(2,1)S(1)}, bf16[1,17,160,128]{3,2,1,0:T(8,128)(2,1)S(1)}, u32[]{:S(2)}, u32[]{:S(2)}) collective-permute-start(bf16[1,17,160,128]{3,2,1,0:T(8,128)(2,1)S(1)} %constant_dynamic-slice_fusion.5), channel_id=1, source_target_pairs={{0,16},{2,18},{4,20},{6,22},{8,24},{10,26},{12,28},{14,30},{16,0},... | collective-permute-start | bytes 2088968 | tf_op jit(solution)/shard_map/ppermute | solution.py:35
  265.6 19.5 %collective-permute-start.40 = (bf16[17,160,128]{2,1,0:T(8,128)(2,1)S(1)}, bf16[17,160,128]{2,1,0:T(8,128)(2,1)S(1)}, u32[]{:S(2)}, u32[]{:S(2)}) collective-permute-start(bf16[17,160,128]{2,1,0:T(8,128)(2,1)S(1)} %fusion.13), channel_id=1, source_target_pairs={{0,6},{2,4},{4,2},{6,0},{8,14},{10,12},{12,10},{14,8},{16,22},{18,... | collective-permute-start | bytes 2088968 | tf_op jit(solution)/shard_map/ppermute | solution.py:35
  268.4 30.8 %collective-permute-start.39 = (bf16[17,160,128]{2,1,0:T(8,128)(2,1)S(1)}, bf16[17,160,128]{2,1,0:T(8,128)(2,1)S(1)}, u32[]{:S(2)}, u32[]{:S(2)}) collective-permute-start(bf16[17,160,128]{2,1,0:T(8,128)(2,1)S(1)} %fusion.13), channel_id=1, source_target_pairs={{0,4},{2,6},{4,0},{6,2},{8,12},{10,14},{12,8},{14,10},{16,20},{18,... | collective-permute-start | bytes 2088968 | tf_op jit(solution)/shard_map/ppermute | solution.py:35
  269.2 30.2 %collective-permute-start.38 = (bf16[17,160,128]{2,1,0:T(8,128)(2,1)S(1)}, bf16[17,160,128]{2,1,0:T(8,128)(2,1)S(1)}, u32[]{:S(2)}, u32[]{:S(2)}) collective-permute-start(bf16[17,160,128]{2,1,0:T(8,128)(2,1)S(1)} %fusion.13), channel_id=1, source_target_pairs={{0,2},{2,0},{4,6},{6,4},{8,10},{10,8},{12,14},{14,12},{16,18},{18,... | collective-permute-start | bytes 2088968 | tf_op jit(solution)/shard_map/ppermute | solution.py:35
  270.9 37.8 %collective-permute-start.11 = (bf16[2,864,128]{2,1,0:T(8,128)(2,1)S(1)}, bf16[2,864,128]{2,1,0:T(8,128)(2,1)S(1)}, u32[]{:S(2)}, u32[]{:S(2)}) collective-permute-start(bf16[2,864,128]{2,1,0:T(8,128)(2,1)S(1)} %fusion.14), channel_id=1, source_target_pairs={{0,4},{2,6},{4,0},{6,2},{8,12},{10,14},{12,8},{14,10},{16,20},{18,... | collective-permute-start | bytes 1327112 | tf_op jit(solution)/shard_map/ppermute | solution.py:35
  285.1 24.8 %collective-permute-start.47 = (bf16[2,864,128]{2,1,0:T(8,128)(2,1)S(1)}, bf16[2,864,128]{2,1,0:T(8,128)(2,1)S(1)}, u32[]{:S(2)}, u32[]{:S(2)}) collective-permute-start(bf16[2,864,128]{2,1,0:T(8,128)(2,1)S(1)} %dynamic-slice_bitcast_fusion.6), channel_id=1, source_target_pairs={{0,8},{2,10},{4,12},{6,14},{8,0},{10,2},{12,4},{14,6},{16,24},{18,... | collective-permute-start | bytes 1327112 | tf_op jit(solution)/shard_map/ppermute | solution.py:35
  300.2 27.4 %collective-permute-start.53 = (bf16[2,2,864,128]{3,2,1,0:T(8,128)(2,1)S(1)}, bf16[2,2,864,128]{3,2,1,0:T(8,128)(2,1)S(1)}, u32[]{:S(2)}, u32[]{:S(2)}) collective-permute-start(bf16[2,2,864,128]{3,2,1,0:T(8,128)(2,1)S(1)} %get-tuple-element.80), channel_id=1, source_target_pairs={{0,4},{2,6},{4,0},{6,2},{8,12},{10,14},{12,8},{14,10},{16,20},{18,... | collective-permute-start | bytes 2654216 | tf_op jit(solution)/shard_map/ppermute | solution.py:35
  303.0 26.3 %collective-permute-start.51 = (bf16[2,2,864,128]{3,2,1,0:T(8,128)(2,1)S(1)}, bf16[2,2,864,128]{3,2,1,0:T(8,128)(2,1)S(1)}, u32[]{:S(2)}, u32[]{:S(2)}) collective-permute-start(bf16[2,2,864,128]{3,2,1,0:T(8,128)(2,1)S(1)} %get-tuple-element.78), channel_id=1, source_target_pairs={{0,2},{2,0},{4,6},{6,4},{8,10},{10,8},{12,14},{14,12},{16,18},{18,... | collective-permute-start | bytes 2654216 | tf_op jit(solution)/shard_map/ppermute | solution.py:35
  310.1 20.2 %collective-permute-start.48 = (bf16[1,864,128]{2,1,0:T(8,128)(2,1)S(1)}, bf16[1,864,128]{2,1,0:T(8,128)(2,1)S(1)}, u32[]{:S(2)}, u32[]{:S(2)}) collective-permute-start(bf16[1,864,128]{2,1,0:T(8,128)(2,1)S(1)} %constant_dynamic-slice_fusion.2), channel_id=1, source_target_pairs={{0,16},{2,18},{4,20},{6,22},{8,24},{10,26},{12,28},{14,30},{16,0},... | collective-permute-start | bytes 663560 | tf_op jit(solution)/shard_map/ppermute | solution.py:35
  330.4 58.0 %collective-permute-start.49 = (bf16[1,864,128]{2,1,0:T(8,128)(2,1)S(1)}, bf16[1,864,128]{2,1,0:T(8,128)(2,1)S(1)}, u32[]{:S(2)}, u32[]{:S(2)}) collective-permute-start(bf16[1,864,128]{2,1,0:T(8,128)(2,1)S(1)} %add_convert_fusion.14), channel_id=1, source_target_pairs={{0,16},{2,18},{4,20},{6,22},{8,24},{10,26},{12,28},{14,30},{16,0},... | collective-permute-start | bytes 663560 | tf_op jit(solution)/shard_map/ppermute | solution.py:35
  330.6 29.6 %collective-permute-start.61 = (bf16[2,2,864,128]{3,2,1,0:T(8,128)(2,1)S(1)}, bf16[2,2,864,128]{3,2,1,0:T(8,128)(2,1)S(1)}, u32[]{:S(2)}, u32[]{:S(2)}) collective-permute-start(bf16[2,2,864,128]{3,2,1,0:T(8,128)(2,1)S(1)} %get-tuple-element.86), channel_id=1, source_target_pairs={{0,4},{2,6},{4,0},{6,2},{8,12},{10,14},{12,8},{14,10},{16,20},{18,... | collective-permute-start | bytes 2654216 | tf_op jit(solution)/shard_map/ppermute | solution.py:35
  339.8 22.7 %collective-permute-start.59 = (bf16[2,2,864,128]{3,2,1,0:T(8,128)(2,1)S(1)}, bf16[2,2,864,128]{3,2,1,0:T(8,128)(2,1)S(1)}, u32[]{:S(2)}, u32[]{:S(2)}) collective-permute-start(bf16[2,2,864,128]{3,2,1,0:T(8,128)(2,1)S(1)} %get-tuple-element.84), channel_id=1, source_target_pairs={{0,2},{2,0},{4,6},{6,4},{8,10},{10,8},{12,14},{14,12},{16,18},{18,... | collective-permute-start | bytes 2654216 | tf_op jit(solution)/shard_map/ppermute | solution.py:35
  347.6 40.7 %collective-permute-start.29 = (bf16[1,864,128]{2,1,0:T(8,128)(2,1)S(1)}, bf16[1,864,128]{2,1,0:T(8,128)(2,1)S(1)}, u32[]{:S(2)}, u32[]{:S(2)}) collective-permute-start(bf16[1,864,128]{2,1,0:T(8,128)(2,1)S(1)} %constant_dynamic-slice_fusion.4), channel_id=1, source_target_pairs={{0,16},{2,18},{4,20},{6,22},{8,24},{10,26},{12,28},{14,30},{16,0},... | collective-permute-start | bytes 663560 | tf_op jit(solution)/shard_map/ppermute | solution.py:35
  360.2 67.2 %collective-permute-start.41 = (bf16[4,17,160,128]{3,2,1,0:T(8,128)(2,1)S(1)}, bf16[4,17,160,128]{3,2,1,0:T(8,128)(2,1)S(1)}, u32[]{:S(2)}, u32[]{:S(2)}) collective-permute-start(bf16[4,17,160,128]{3,2,1,0:T(8,128)(2,1)S(1)} %pad_maximum_fusion.1.refs_0_), channel_id=1, source_target_pairs={{0,1},{1,0},{2,3},{3,2},{4,5},{5,4},{6,7},{7,6},{8,9},{9,8},{10,11... | collective-permute-start | bytes 8355848 | tf_op jit(solution)/shard_map/ppermute | solution.py:35
  388.4 57.7 %collective-permute-start.50 = (bf16[2,864,128]{2,1,0:T(8,128)(2,1)S(1)}, bf16[2,864,128]{2,1,0:T(8,128)(2,1)S(1)}, u32[]{:S(2)}, u32[]{:S(2)}) collective-permute-start(bf16[2,864,128]{2,1,0:T(8,128)(2,1)S(1)} %pad_maximum_fusion.11.b_ref), channel_id=1, source_target_pairs={{0,8},{2,10},{4,12},{6,14},{8,0},{10,2},{12,4},{14,6},{16,24},{18,... | collective-permute-start | bytes 1327112 | tf_op jit(solution)/shard_map/ppermute | solution.py:35
  390.5 36.8 %collective-permute-start.58 = (bf16[2,864,128]{2,1,0:T(8,128)(2,1)S(1)}, bf16[2,864,128]{2,1,0:T(8,128)(2,1)S(1)}, u32[]{:S(2)}, u32[]{:S(2)}) collective-permute-start(bf16[2,864,128]{2,1,0:T(8,128)(2,1)S(1)} %pad_maximum_fusion.12.b_ref), channel_id=1, source_target_pairs={{0,8},{2,10},{4,12},{6,14},{8,0},{10,2},{12,4},{14,6},{16,24},{18,... | collective-permute-start | bytes 1327112 | tf_op jit(solution)/shard_map/ppermute | solution.py:35
  403.6 59.6 %collective-permute-start.42 = (bf16[2,864,128]{2,1,0:T(8,128)(2,1)S(1)}, bf16[2,864,128]{2,1,0:T(8,128)(2,1)S(1)}, u32[]{:S(2)}, u32[]{:S(2)}) collective-permute-start(bf16[2,864,128]{2,1,0:T(8,128)(2,1)S(1)} %pad_maximum_fusion.10.b_ref), channel_id=1, source_target_pairs={{0,8},{2,10},{4,12},{6,14},{8,0},{10,2},{12,4},{14,6},{16,24},{18,... | collective-permute-start | bytes 1327112 | tf_op jit(solution)/shard_map/ppermute | solution.py:35
  405.7 74.8 %collective-permute-start.64 = (bf16[1,864,128]{2,1,0:T(8,128)(2,1)S(1)}, bf16[1,864,128]{2,1,0:T(8,128)(2,1)S(1)}, u32[]{:S(2)}, u32[]{:S(2)}) collective-permute-start(bf16[1,864,128]{2,1,0:T(8,128)(2,1)S(1)} %constant_dynamic-slice_fusion), channel_id=1, source_target_pairs={{0,16},{2,18},{4,20},{6,22},{8,24},{10,26},{12,28},{14,30},{16,0},... | collective-permute-start | bytes 663560 | tf_op jit(solution)/shard_map/ppermute | solution.py:35
  (48 other events, 383.3 us)
